TPU v7x, 256 devices: a whole 4x4x8 slice. The times are simulated.
256 devices in a mesh: row: 16 (over y, z_lo, core), col: 16 (over z_hi, x).
Axes of the slice: x: 4, y: 4, z: 8 (z_hi: 4, z_lo: 2; z = z_hi * 2 + z_lo), core: 2. Of those that a mesh axis runs over, the one named last changes fastest.
Arguments:
- layer_input: bfloat16 [2048, 12288], P('col', 'row'), may hold values from -6 to 6
- out_grad: bfloat16 [2048, 12288], P('col', 'row'), may hold values from -6 to 6
- preact: bfloat16 [2048, 16384], P('row', 'col'), may hold values from -6 to 6
- weight_in: bfloat16 [12288, 16384], P('row', 'col'), may hold values from -0.0546875 to 0.0546875
- weight_out: bfloat16 [16384, 12288], P('col', 'row'), may hold values from -0.046875 to 0.046875
Outputs:
- input_grad: bfloat16 [2048, 12288], P('col', 'row')
- weight_in_grad: float32 [12288, 16384], P('row', 'col')
- weight_out_grad: float32 [16384, 12288], P('col', 'row')
All inputs are finite; a program needn't handle non-finite values.
Results may differ from a plain program's by a relative error of at most 0.019.
Values may be sent and summed in bfloat16 or wider, within the bound.
No kernel may reach another device: no remote copies, remote signals or barrier semaphores. Data moves between devices by JAX's collectives and lax.ppermute only.
A program may use at most 128 MiB of HBM per device.

v0:
```python
import math

import jax
import jax.numpy as jnp
from jax import lax
from jax.sharding import PartitionSpec as P

BF = jnp.bfloat16
F32 = jnp.float32


def gelu_parts(h):
    c = math.sqrt(2.0 / math.pi)
    t = jnp.tanh(c * (h + 0.044715 * h * h * h))
    value = 0.5 * h * (1.0 + t)
    slope = 0.5 * (1.0 + t) + 0.5 * h * (1.0 - t * t) * c * (1.0 + 3.0 * 0.044715 * h * h)
    return (value, slope)


def token_contract(left, right):
    return lax.dot_general(left, right, (((0,), (0,)), ((), ())), preferred_element_type=F32)


def width_contract(left, right):
    return lax.dot_general(left, right, (((1,), (1,)), ((), ())), preferred_element_type=F32)


def move(v, axis, span, stride, step):
    def to(i):
        at = (i // stride) % span
        return i + (((at + step) % span) - at) * stride

    return lax.ppermute(v, axis, [(i, to(i)) for i in range(16)])


def swap(v, axis, bit):
    return lax.ppermute(v, axis, [(i, i ^ bit) for i in range(16)])


def around_x(v, first):
    def to(i):
        return i ^ (1 if (i // 16 % 2 == 0) == first else 3)

    return lax.ppermute(v, ("row", "col"), [(i, to(i)) for i in range(256)])


def around_y(v, first):
    def to(i):
        return i ^ (4 if (i % 2 == 0) == first else 12)

    return lax.ppermute(v, "row", [(i, to(i)) for i in range(16)])


def along_x(v, d):
    return move(v, "col", 4, 1, d)


def along_zh(v, d):
    return move(v, "col", 4, 4, d)


def along_y(v, d):
    return move(v, "row", 4, 4, d)


def along_zl(v):
    return move(v, "row", 2, 2, 1)


def along_core(v):
    return move(v, "row", 2, 1, 1)


STEPS = (1, -1, 2)


def put(whole, piece, at, dim):
    return lax.dynamic_update_slice_in_dim(whole, jnp.expand_dims(piece, dim), at, dim)


def take(whole, at, dim):
    return lax.dynamic_index_in_dim(whole, at, dim, keepdims=False)


def spread(own, copies, dim):
    shape = list(own.shape)
    shape.insert(dim, copies)
    return jnp.broadcast_to(jnp.expand_dims(own, dim), shape)


def gather4(shift, own, me, dim, hold=()):
    got = [(d, shift(own, d)) for d in STEPS]
    whole = after(spread(own, 4, dim), *hold)
    for d, piece in got:
        whole = put(whole, piece, (me - d) % 4, dim)
    return whole


def place4(own, near, far, me, core, dim, hold=()):
    first = 1 + 2 * core
    whole = put(after(spread(own, 4, dim), *hold), near, me ^ first, dim)
    return put(put(whole, far[0], me ^ (4 - first), dim), far[1], me ^ 2, dim)


def blocks_away(whole, me, dim):
    return [take(whole, (me + d) % 4, dim).astype(BF) for d in STEPS]


def scatter4(shift, whole, away, me, dim, hold=()):
    got = [shift(block, d) for block, d in zip(away, STEPS)]
    total = after(take(whole, me, dim), *hold)
    for piece in got:
        total = total + piece.astype(F32)
    return total


def pair2(own, other, me, dim, hold=()):
    return put(after(spread(own, 2, dim), *hold), other, 1 - me, dim)


def after(v, *others):
    return lax.optimization_barrier((v, *others))[0] if others else v


CHUNKS = 2


def local(layer_input, out_grad, preact, weight_in, weight_out):
    col, row = lax.axis_index("col"), lax.axis_index("row")
    zh, x = col // 4, col % 4
    y, zl, core = row // 4, (row // 2) % 2, row % 2
    tokens, width = out_grad.shape
    hidden = preact.shape[1]
    n = tokens // CHUNKS

    def core_sum(og):
        og5 = og.reshape(2, 2, 4, n, width)

        def grad_for(c):
            return width_contract(take(og5, c, 1).reshape(8 * n, width), weight_out)

        away = along_core(grad_for(1 - core).astype(BF))
        mine = grad_for(core) + away.astype(F32)
        return mine.reshape(2, 4, n, hidden)

    def pre_grad(sent, k):
        grad_act = sent.astype(F32) + along_zl(sent).astype(F32)
        return (grad_act * slope[:, k * n : (k + 1) * n]).astype(BF)

    def y_gather(share, hold):
        near = around_y(share, True)
        far = around_y(jnp.stack([share, near]), False)
        return place4(share, near, far, y, core, 1, hold)

    def partials(gp):
        return width_contract(gp.reshape(16 * n, hidden), weight_in).reshape(4, 4, n, width)

    def chunk_of(v, k):
        return v[:, :, k * n : (k + 1) * n].reshape(16 * n, v.shape[-1])

    by_z = gather4(along_zh, out_grad, zh, 0)
    activ = gelu_parts(preact.astype(F32))[0].astype(BF)
    activ_panel = lax.all_gather(activ, "row", axis=0, tiled=True)
    pre_pair = pair2(preact, along_zl(preact), zl, 0)
    slope = gelu_parts(pre_pair.astype(F32))[1]

    low = pair2(layer_input, swap(after(layer_input, by_z), "col", 4), zh % 2, 0)
    near1 = around_x(by_z[:, n:], True)
    both1 = jnp.stack([by_z[:, n:], near1])
    og0 = gather4(along_x, by_z[:, :n], x, 0, hold=(slope, low, both1))
    mine0 = core_sum(og0)
    away0 = blocks_away(mine0, y, 1)
    far1 = around_x(after(both1, og0), False)
    og1 = place4(by_z[:, n:], near1, far1, x, core, 0, hold=(*away0, activ_panel))
    def out_term(k, og, *first):
        activ_x = after(activ_panel, *first).reshape(4, 4, tokens, hidden).transpose(1, 0, 2, 3)
        return token_contract(chunk_of(activ_x, k), og.reshape(16 * n, width))

    def in_term(k, gp, *first):
        return token_contract(chunk_of(after(input_panel, *first), k), gp.reshape(16 * n, hidden))

    mine1 = core_sum(og1)
    away1 = blocks_away(mine1, y, 1)
    input_z = pair2(low, swap(after(low, og1), "col", 12), zh // 2, 0, hold=tuple(away1))
    input_z = input_z.reshape(4, tokens, width)
    input_near = around_x(input_z, True)
    input_far = around_x(jnp.stack([input_z, input_near]), False)
    input_panel = place4(input_z, input_near, input_far, x, core, 0)
    pair0 = scatter4(along_y, mine0, away0, y, 1, hold=tuple(away1))
    gpre0 = pre_grad(pair0.astype(BF), 0)
    pair1 = scatter4(along_y, mine1, [after(v, pair0) for v in away1], y, 1, hold=(gpre0,))
    sent1 = pair1.astype(BF)
    weight_out_grad = out_term(0, og0, sent1)
    gpre1 = pre_grad(sent1, 1)
    half0 = y_gather(after(gpre0, pair1), hold=(gpre1, weight_out_grad, input_panel))
    gp0 = pair2(half0, along_core(half0), core, 1)
    part0 = partials(gp0)
    far0 = blocks_away(part0, x, 0)
    half1 = y_gather(after(gpre1, half0), hold=tuple(far0))
    gp1 = pair2(half1, along_core(half1), core, 1)
    part1 = partials(gp1)
    far1 = blocks_away(part1, x, 0)
    weight_out_grad = weight_out_grad + out_term(1, og1, *far1)
    weight_in_grad = in_term(0, gp0, *far1)
    by_x0 = scatter4(along_x, part0, far0, x, 0, hold=(*far1, weight_out_grad, weight_in_grad))
    up0 = blocks_away(by_x0, zh, 0)
    weight_in_grad = weight_in_grad + in_term(1, gp1, *up0)
    out0 = scatter4(along_zh, by_x0, up0, zh, 0).astype(BF)
    by_x1 = scatter4(along_x, part1, [after(v, by_x0) for v in far1], x, 0, hold=(weight_in_grad,))
    up1 = blocks_away(by_x1, zh, 0)
    out1 = scatter4(along_zh, by_x1, up1, zh, 0).astype(BF)
    input_grad = jnp.concatenate([out0, out1], axis=0)
    return (input_grad, weight_in_grad, weight_out_grad)


def solution(mesh):
    placed = (P("col", "row"), P("col", "row"), P("row", "col"), P("row", "col"), P("col", "row"))
    return jax.shard_map(
        local,
        mesh=mesh,
        in_specs=placed,
        out_specs=(P("col", "row"), P("row", "col"), P("col", "row")),
        check_vma=False,
    )
```

profile of v0, /device:TPU:1, one launch (start us, length us, event | category | flops | bytes accessed | tf_op | source)
XLA Modules:
  0.0 260.6 jit_solution(2595547619972111197)
XLA Ops:
  7.2 2.0 fusion.21
  9.2 3.9 %collective-permute-start = (bf16[128,768]{1,0:T(8,128)(2,1)}, bf16[128,768]{1,0:T(8,128)(2,1)S(1)}, u32[]{:S(2)}, u32[]{:S(2)}) collective-permute-start(bf16[128,768]{1,0:T(8,128)(2,1)} %param.6), channel_id=1, source_target_pairs={{0,4},{1,5},{2,6},{3,7},{4,8},{5,9},{6,10},{7,11},{8,12},{9,13},{1... | collective-permute-start | bytes 589832 | tf_op jit(solution)/shard_map/ppermute | solution.py:33
  13.1 5.1 %collective-permute-start.2 = (bf16[128,768]{1,0:T(8,128)(2,1)}, bf16[128,768]{1,0:T(8,128)(2,1)S(1)}, u32[]{:S(2)}, u32[]{:S(2)}) collective-permute-start(bf16[128,768]{1,0:T(8,128)(2,1)} %param.6), channel_id=1, source_target_pairs={{0,8},{1,9},{2,10},{3,11},{4,12},{5,13},{6,14},{7,15},{8,0},{9,1},... | collective-permute-start | bytes 589832 | tf_op jit(solution)/shard_map/ppermute | solution.py:33
  18.2 2.4 collective-permute-start.1
  22.6 11.9 %collective-permute-done.1 = bf16[128,768]{1,0:T(8,128)(2,1)S(1)} collective-permute-done((bf16[128,768]{1,0:T(8,128)(2,1)}, bf16[128,768]{1,0:T(8,128)(2,1)S(1)}, u32[]{:S(2)}, u32[]{:S(2)}) %collective-permute-start.1) | collective-permute-done | bytes 196640 | tf_op jit(solution)/shard_map/ppermute | solution.py:33
  34.7 2.8 %collective-permute-start.8 = (bf16[4,64,768]{2,1,0:T(8,128)(2,1)S(1)}, bf16[4,64,768]{2,1,0:T(8,128)(2,1)S(1)}, u32[]{:S(2)}, u32[]{:S(2)}) collective-permute-start(bf16[4,64,768]{2,1,0:T(8,128)(2,1)S(1)} %get-tuple-element.75), channel_id=1, source_target_pairs={{0,2},{1,3},{2,0},{3,1},{4,6},{5,7},{6,4},{7,5},{8,10},{9,11},{10,... | collective-permute-start | bytes 1179656 | tf_op jit(solution)/shard_map/ppermute | solution.py:33
  39.0 3.8 %collective-permute-start.4 = (bf16[128,768]{1,0:T(8,128)(2,1)S(1)}, bf16[128,768]{1,0:T(8,128)(2,1)S(1)}, u32[]{:S(2)}, u32[]{:S(2)}) collective-permute-start(bf16[128,768]{1,0:T(8,128)(2,1)S(1)} %copy-done.20), channel_id=1, source_target_pairs={{0,4},{1,5},{2,6},{3,7},{4,0},{5,1},{6,2},{7,3},{8,12},{9,13},{10,... | collective-permute-start | bytes 589832 | tf_op jit(solution)/shard_map/ppermute | solution.py:37
  42.8 13.6 %collective-permute-done.3 = bf16[128,1024]{1,0:T(8,128)(2,1)S(1)} collective-permute-done((bf16[128,1024]{1,0:T(8,128)(2,1)}, bf16[128,1024]{1,0:T(8,128)(2,1)S(1)}, u32[]{:S(2)}, u32[]{:S(2)}) %collective-permute-start.3) | collective-permute-done | bytes 262176 | tf_op jit(solution)/shard_map/ppermute | solution.py:33
  56.3 2.5 collective-permute-start.5
  59.0 1.7 fusion.18
  60.7 3.5 %collective-permute-done.5 = bf16[4,64,768]{2,1,0:T(8,128)(2,1)S(1)} collective-permute-done((bf16[4,64,768]{2,1,0:T(8,128)(2,1)S(1)}, bf16[4,64,768]{2,1,0:T(8,128)(2,1)S(1)}, u32[]{:S(2)}, u32[]{:S(2)}) %collective-permute-start.5) | collective-permute-done | bytes 393248 | tf_op jit(solution)/shard_map/ppermute | solution.py:44
  67.2 2.0 convolution_convert_fusion.1
  69.2 1.7 collective-permute-start.9
  70.9 1.2 collective-permute-start.10
  72.1 1.4 collective-permute-done.9
  73.5 2.5 convert_add_fusion.2
  76.0 1.3 copy-done.18
  79.5 2.8 %collective-permute-done.10 = bf16[2,4,64,768]{3,2,1,0:T(8,128)(2,1)} collective-permute-done((bf16[2,4,64,768]{3,2,1,0:T(8,128)(2,1)}, bf16[2,4,64,768]{3,2,1,0:T(8,128)(2,1)}, u32[]{:S(2)}, u32[]{:S(2)}) %collective-permute-start.10) | collective-permute-done | bytes 786464 | tf_op jit(solution)/shard_map/ppermute | solution.py:44
  84.4 1.2 copy-done.8
  86.7 2.0 convolution_convert_fusion
  88.6 2.3 collective-permute-start.11
  91.0 3.4 %collective-permute-start.12 = (bf16[2,64,1024]{2,1,0:T(8,128)(2,1)}, bf16[2,64,1024]{2,1,0:T(8,128)(2,1)S(1)}, u32[]{:S(2)}, u32[]{:S(2)}) collective-permute-start(bf16[2,64,1024]{2,1,0:T(8,128)(2,1)} %get-tuple-element.61), channel_id=1, source_target_pairs={{0,64},{16,80},{32,96},{48,112},{64,128},{80,144},{96,160},{112,17... | collective-permute-start | bytes 786440 | tf_op jit(solution)/shard_map/ppermute | solution.py:33
  94.5 2.3 collective-permute-start.20
  96.8 2.5 convert_add_fusion.1
  100.4 12.3 %collective-permute-done.20 = bf16[2,128,768]{2,1,0:T(8,128)(2,1)S(1)} collective-permute-done((bf16[2,128,768]{2,1,0:T(8,128)(2,1)S(1)}, bf16[2,128,768]{2,1,0:T(8,128)(2,1)S(1)}, u32[]{:S(2)}, u32[]{:S(2)}) %collective-permute-start.20) | collective-permute-done | bytes 393248 | tf_op jit(solution)/shard_map/ppermute | solution.py:37
  112.7 2.3 collective-permute-start.21
  116.2 4.0 %collective-permute-start.15 = (bf16[2,64,1024]{2,1,0:T(8,128)(2,1)S(1)}, bf16[2,64,1024]{2,1,0:T(8,128)(2,1)}, u32[]{:S(2)}, u32[]{:S(2)}) collective-permute-start(bf16[2,64,1024]{2,1,0:T(8,128)(2,1)S(1)} %convert_add_fusion.7), channel_id=1, source_target_pairs={{0,32},{16,48},{32,0},{48,16},{64,96},{80,112},{96,64},{112,80},{1... | collective-permute-start | bytes 786440 | tf_op jit(solution)/shard_map/ppermute | solution.py:33
  120.2 1.4 collective-permute-start.16
  121.6 1.3 collective-permute-start.17
  124.6 1.8 collective-permute-done.15
  127.8 7.6 %collective-permute-done.16 = bf16[2,64,1024]{2,1,0:T(8,128)(2,1)S(1)} collective-permute-done((bf16[2,64,1024]{2,1,0:T(8,128)(2,1)}, bf16[2,64,1024]{2,1,0:T(8,128)(2,1)S(1)}, u32[]{:S(2)}, u32[]{:S(2)}) %collective-permute-start.16) | collective-permute-done | bytes 262176 | tf_op jit(solution)/shard_map/ppermute | solution.py:33
  135.7 2.8 %collective-permute-start.23 = (bf16[2,64,1024]{2,1,0:T(8,128)(2,1)S(1)}, bf16[2,64,1024]{2,1,0:T(8,128)(2,1)S(1)}, u32[]{:S(2)}, u32[]{:S(2)}) collective-permute-start(bf16[2,64,1024]{2,1,0:T(8,128)(2,1)S(1)} %fusion.26), channel_id=1, source_target_pairs={{0,64},{16,208},{32,96},{48,240},{64,0},{80,144},{96,32},{112,176}... | collective-permute-start | bytes 786440 | tf_op jit(solution)/shard_map/ppermute | solution.py:51
  139.1 3.6 %fusion.4 = f32[1024,768]{1,0:T(8,128)} fusion(bf16[4,4,64,768]{3,2,1,0:T(8,128)(2,1)S(1)} %bitcast_dynamic-update-slice_fusion.3, bf16[4,4,128,1024]{3,2,1,0:T(8,128)(2,1)S(1)} %bitcast.210), kind=kOutput, calls=%fused_computation.16 | convolution fusion | flops 1610612736 | bytes 6815744 | tf_op jit(solution)/shard_map/dot_general | solution.py:21
  142.7 14.5 %collective-permute-start.24 = (bf16[2,2,64,1024]{3,2,1,0:T(8,128)(2,1)S(1)}, bf16[2,2,64,1024]{3,2,1,0:T(8,128)(2,1)S(1)}, u32[]{:S(2)}, u32[]{:S(2)}) collective-permute-start(bf16[2,2,64,1024]{3,2,1,0:T(8,128)(2,1)S(1)} %pad_maximum_fusion.2), channel_id=1, source_target_pairs={{0,192},{16,80},{32,224},{48,112},{64,128},{80,16},{96,160},{112,4... | collective-permute-start | bytes 1572872 | tf_op jit(solution)/shard_map/ppermute | solution.py:51
  160.5 5.0 %collective-permute-done.24 = bf16[2,2,64,1024]{3,2,1,0:T(8,128)(2,1)S(1)} collective-permute-done((bf16[2,2,64,1024]{3,2,1,0:T(8,128)(2,1)S(1)}, bf16[2,2,64,1024]{3,2,1,0:T(8,128)(2,1)S(1)}, u32[]{:S(2)}, u32[]{:S(2)}) %collective-permute-start.24) | collective-permute-done | bytes 524320 | tf_op jit(solution)/shard_map/ppermute | solution.py:51
  167.0 1.9 collective-permute-start.25
  168.8 3.0 %collective-permute-start.26 = (bf16[2,64,1024]{2,1,0:T(8,128)(2,1)S(1)}, bf16[2,64,1024]{2,1,0:T(8,128)(2,1)}, u32[]{:S(2)}, u32[]{:S(2)}) collective-permute-start(bf16[2,64,1024]{2,1,0:T(8,128)(2,1)S(1)} %fusion.25), channel_id=1, source_target_pairs={{0,64},{16,208},{32,96},{48,240},{64,0},{80,144},{96,32},{112,176}... | collective-permute-start | bytes 786440 | tf_op jit(solution)/shard_map/ppermute | solution.py:51
  171.8 3.9 %collective-permute-done.26 = bf16[2,64,1024]{2,1,0:T(8,128)(2,1)} collective-permute-done((bf16[2,64,1024]{2,1,0:T(8,128)(2,1)S(1)}, bf16[2,64,1024]{2,1,0:T(8,128)(2,1)}, u32[]{:S(2)}, u32[]{:S(2)}) %collective-permute-start.26) | collective-permute-done | bytes 262176 | tf_op jit(solution)/shard_map/ppermute | solution.py:51
  176.8 1.6 broadcast_in_dim.130
  178.3 1.3 bitcast_dynamic-update-slice_fusion.1
  179.7 1.8 fusion.11
  183.9 1.7 bitcast_dynamic-update-slice_fusion.6
  187.1 2.8 %collective-permute-start.28 = (bf16[2,4,64,1024]{3,2,1,0:T(8,128)(2,1)}, bf16[2,4,64,1024]{3,2,1,0:T(8,128)(2,1)}, u32[]{:S(2)}, u32[]{:S(2)}) collective-permute-start(bf16[2,4,64,1024]{3,2,1,0:T(8,128)(2,1)} %fusion.39), channel_id=1, source_target_pairs={{0,16},{16,0},{32,48},{48,32},{64,80},{80,64},{96,112},{112,96},{1... | collective-permute-start | bytes 3145736 | tf_op jit(solution)/shard_map/ppermute | solution.py:33
  190.0 1.5 collective-permute-start.30
  192.5 1.5 broadcast_in_dim.134
  194.0 1.3 bitcast_dynamic-update-slice_fusion
  195.3 1.8 fusion.9
  197.3 1.5 dynamic-slice_bitcast_fusion
  201.9 3.7 %bitcast_add_fusion = f32[1024,768]{1,0:T(8,128)} fusion(f32[1024,768]{1,0:T(8,128)S(1)} %copy-done.24, bf16[4,4,64,768]{3,2,1,0:T(8,128)(2,1)S(1)} %copy-done.9, bf16[4,4,128,1024]{3,2,1,0:T(8,128)(2,1)S(1)} %bitcast.209), kind=kOutput, calls=%fused_computation.2 | convolution fusion | flops 1611399168 | bytes 9961472 | tf_op jit(solution)/shard_map/dot_general | solution.py:21
  205.7 1.5 copy-done.5
  207.2 1.8 fusion.55
  209.5 1.5 collective-permute-done.29
  211.3 2.4 collective-permute-start.34
  213.7 1.5 collective-permute-start.33
  215.3 1.2 collective-permute-start.36
  217.2 3.6 %convolution_add_fusion = f32[768,1024]{1,0:T(8,128)} fusion(f32[768,1024]{1,0:T(8,128)S(1)} %fusion.55, bf16[1024,768]{1,0:T(8,128)(2,1)S(1)} %bitcast.216, bf16[1024,1024]{1,0:T(8,128)(2,1)S(1)} %bitcast.215), kind=kOutput, calls=%fused_computation.17 | convolution fusion | flops 1611399168 | bytes 9961472 | tf_op jit(solution)/shard_map/dot_general | solution.py:21
  220.8 4.1 %collective-permute-done.36 = bf16[4,64,768]{2,1,0:T(8,128)(2,1)S(1)} collective-permute-done((bf16[4,64,768]{2,1,0:T(8,128)(2,1)S(1)}, bf16[4,64,768]{2,1,0:T(8,128)(2,1)S(1)}, u32[]{:S(2)}, u32[]{:S(2)}) %collective-permute-start.36) | collective-permute-done | bytes 393248 | tf_op jit(solution)/shard_map/ppermute | solution.py:33
  225.8 1.6 collective-permute-done.37
  227.4 9.5 %collective-permute-done.35 = bf16[4,64,768]{2,1,0:T(8,128)(2,1)S(1)} collective-permute-done((bf16[4,64,768]{2,1,0:T(8,128)(2,1)S(1)}, bf16[4,64,768]{2,1,0:T(8,128)(2,1)S(1)}, u32[]{:S(2)}, u32[]{:S(2)}) %collective-permute-start.35) | collective-permute-done | bytes 393248 | tf_op jit(solution)/shard_map/ppermute | solution.py:33
  237.1 1.8 collective-permute-start.38
  238.9 2.2 collective-permute-start.40
  241.1 3.2 %collective-permute-start.39 = (bf16[64,768]{1,0:T(8,128)(2,1)S(1)}, bf16[64,768]{1,0:T(8,128)(2,1)S(1)}, u32[]{:S(2)}, u32[]{:S(2)}) collective-permute-start(bf16[64,768]{1,0:T(8,128)(2,1)S(1)} %get-tuple-element.69), channel_id=1, source_target_pairs={{0,12},{1,13},{2,14},{3,15},{4,0},{5,1},{6,2},{7,3},{8,4},{9,5},{1... | collective-permute-start | bytes 294920 | tf_op jit(solution)/shard_map/ppermute | solution.py:33
  244.4 3.7 %collective-permute-done.40 = bf16[64,768]{1,0:T(8,128)(2,1)S(1)} collective-permute-done((bf16[64,768]{1,0:T(8,128)(2,1)S(1)}, bf16[64,768]{1,0:T(8,128)(2,1)S(1)}, u32[]{:S(2)}, u32[]{:S(2)}) %collective-permute-start.40) | collective-permute-done | bytes 98336 | tf_op jit(solution)/shard_map/ppermute | solution.py:33
  248.1 4.7 %collective-permute-done.39 = bf16[64,768]{1,0:T(8,128)(2,1)S(1)} collective-permute-done((bf16[64,768]{1,0:T(8,128)(2,1)S(1)}, bf16[64,768]{1,0:T(8,128)(2,1)S(1)}, u32[]{:S(2)}, u32[]{:S(2)}) %collective-permute-start.39) | collective-permute-done | bytes 98336 | tf_op jit(solution)/shard_map/ppermute | solution.py:33
  (146 shorter events, 36.0 us)
Async XLA Ops:
  7.2 60.0 %copy-start = (bf16[1024,768]{1,0:T(8,128)(2,1)S(1)}, bf16[1024,768]{1,0:T(8,128)(2,1)}, u32[]{:S(2)}) copy-start(bf16[1024,768]{1,0:T(8,128)(2,1)} %param.9) | copy-start | bytes 4718596
  7.2 71.1 %all-gather.2.cloned.1.call-start = ((), (), s32[]{:S(2)}) async-start(), calls=%async_computation | async-start | bytes 4456448 | tf_op jit(solution)/shard_map/all_gather | solution.py:163
  9.2 12.4 %collective-permute-start = (bf16[128,768]{1,0:T(8,128)(2,1)}, bf16[128,768]{1,0:T(8,128)(2,1)S(1)}, u32[]{:S(2)}, u32[]{:S(2)}) collective-permute-start(bf16[128,768]{1,0:T(8,128)(2,1)} %param.6), channel_id=1, source_target_pairs={{0,4},{1,5},{2,6},{3,7},{4,8},{5,9},{6,10},{7,11},{8,12},{9,13},{1... | collective-permute-start | bytes 589832 | tf_op jit(solution)/shard_map/ppermute | solution.py:33
  13.1 21.4 %collective-permute-start.2 = (bf16[128,768]{1,0:T(8,128)(2,1)}, bf16[128,768]{1,0:T(8,128)(2,1)S(1)}, u32[]{:S(2)}, u32[]{:S(2)}) collective-permute-start(bf16[128,768]{1,0:T(8,128)(2,1)} %param.6), channel_id=1, source_target_pairs={{0,8},{1,9},{2,10},{3,11},{4,12},{5,13},{6,14},{7,15},{8,0},{9,1},... | collective-permute-start | bytes 589832 | tf_op jit(solution)/shard_map/ppermute | solution.py:33
  18.2 16.3 %collective-permute-start.1 = (bf16[128,768]{1,0:T(8,128)(2,1)}, bf16[128,768]{1,0:T(8,128)(2,1)S(1)}, u32[]{:S(2)}, u32[]{:S(2)}) collective-permute-start(bf16[128,768]{1,0:T(8,128)(2,1)} %param.6), channel_id=1, source_target_pairs={{0,12},{1,13},{2,14},{3,15},{4,0},{5,1},{6,2},{7,3},{8,4},{9,5},{1... | collective-permute-start | bytes 589832 | tf_op jit(solution)/shard_map/ppermute | solution.py:33
  20.6 35.7 %collective-permute-start.3 = (bf16[128,1024]{1,0:T(8,128)(2,1)}, bf16[128,1024]{1,0:T(8,128)(2,1)S(1)}, u32[]{:S(2)}, u32[]{:S(2)}) collective-permute-start(bf16[128,1024]{1,0:T(8,128)(2,1)} %param.7), channel_id=1, source_target_pairs={{0,32},{16,48},{32,0},{48,16},{64,96},{80,112},{96,64},{112,80},{1... | collective-permute-start | bytes 786440 | tf_op jit(solution)/shard_map/ppermute | solution.py:33
  21.3 17.6 %copy-start.20 = (bf16[128,768]{1,0:T(8,128)(2,1)S(1)}, bf16[128,768]{1,0:T(8,128)(2,1)}, u32[]{:S(2)}) copy-start(bf16[128,768]{1,0:T(8,128)(2,1)} %param.5) | copy-start | bytes 589828
  21.3 37.5 %copy-start.17 = (bf16[128,1024]{1,0:T(8,128)(2,1)S(1)}, bf16[128,1024]{1,0:T(8,128)(2,1)}, u32[]{:S(2)}) copy-start(bf16[128,1024]{1,0:T(8,128)(2,1)} %param.7) | copy-start | bytes 786436
  34.6 26.1 %copy-start.21 = (bf16[128,768]{1,0:T(8,128)(2,1)S(1)}, bf16[128,768]{1,0:T(8,128)(2,1)}, u32[]{:S(2)}) copy-start(bf16[128,768]{1,0:T(8,128)(2,1)} %param.5) | copy-start | bytes 589828
  34.7 29.5 %copy-start.15 = (bf16[4,64,768]{2,1,0:T(8,128)(2,1)}, bf16[4,64,768]{2,1,0:T(8,128)(2,1)S(1)}, u32[]{:S(2)}) copy-start(bf16[4,64,768]{2,1,0:T(8,128)(2,1)S(1)} %get-tuple-element.74) | copy-start | bytes 1179652
  34.7 31.5 %collective-permute-start.8 = (bf16[4,64,768]{2,1,0:T(8,128)(2,1)S(1)}, bf16[4,64,768]{2,1,0:T(8,128)(2,1)S(1)}, u32[]{:S(2)}, u32[]{:S(2)}) collective-permute-start(bf16[4,64,768]{2,1,0:T(8,128)(2,1)S(1)} %get-tuple-element.75), channel_id=1, source_target_pairs={{0,2},{1,3},{2,0},{3,1},{4,6},{5,7},{6,4},{7,5},{8,10},{9,11},{10,... | collective-permute-start | bytes 1179656 | tf_op jit(solution)/shard_map/ppermute | solution.py:33
  37.5 28.6 %collective-permute-start.7 = (bf16[4,64,768]{2,1,0:T(8,128)(2,1)S(1)}, bf16[4,64,768]{2,1,0:T(8,128)(2,1)S(1)}, u32[]{:S(2)}, u32[]{:S(2)}) collective-permute-start(bf16[4,64,768]{2,1,0:T(8,128)(2,1)S(1)} %get-tuple-element.75), channel_id=1, source_target_pairs={{0,3},{1,0},{2,1},{3,2},{4,7},{5,4},{6,5},{7,6},{8,11},{9,8},{10,9... | collective-permute-start | bytes 1179656 | tf_op jit(solution)/shard_map/ppermute | solution.py:33
  38.4 27.7 %collective-permute-start.6 = (bf16[4,64,768]{2,1,0:T(8,128)(2,1)S(1)}, bf16[4,64,768]{2,1,0:T(8,128)(2,1)S(1)}, u32[]{:S(2)}, u32[]{:S(2)}) collective-permute-start(bf16[4,64,768]{2,1,0:T(8,128)(2,1)S(1)} %get-tuple-element.75), channel_id=1, source_target_pairs={{0,1},{1,2},{2,3},{3,0},{4,5},{5,6},{6,7},{7,4},{8,9},{9,10},{10,1... | collective-permute-start | bytes 1179656 | tf_op jit(solution)/shard_map/ppermute | solution.py:33
  39.0 21.7 %collective-permute-start.4 = (bf16[128,768]{1,0:T(8,128)(2,1)S(1)}, bf16[128,768]{1,0:T(8,128)(2,1)S(1)}, u32[]{:S(2)}, u32[]{:S(2)}) collective-permute-start(bf16[128,768]{1,0:T(8,128)(2,1)S(1)} %copy-done.20), channel_id=1, source_target_pairs={{0,4},{1,5},{2,6},{3,7},{4,0},{5,1},{6,2},{7,3},{8,12},{9,13},{10,... | collective-permute-start | bytes 589832 | tf_op jit(solution)/shard_map/ppermute | solution.py:37
  56.3 7.8 %collective-permute-start.5 = (bf16[4,64,768]{2,1,0:T(8,128)(2,1)S(1)}, bf16[4,64,768]{2,1,0:T(8,128)(2,1)S(1)}, u32[]{:S(2)}, u32[]{:S(2)}) collective-permute-start(bf16[4,64,768]{2,1,0:T(8,128)(2,1)S(1)} %get-tuple-element.74), channel_id=1, source_target_pairs={{0,1},{1,0},{2,3},{3,2},{4,5},{5,4},{6,7},{7,6},{8,9},{9,8},{10,11... | collective-permute-start | bytes 1179656 | tf_op jit(solution)/shard_map/ppermute | solution.py:44
  69.2 4.3 %collective-permute-start.9 = (bf16[512,1024]{1,0:T(8,128)(2,1)}, bf16[512,1024]{1,0:T(8,128)(2,1)}, u32[]{:S(2)}, u32[]{:S(2)}) collective-permute-start(bf16[512,1024]{1,0:T(8,128)(2,1)} %convolution_convert_fusion.1), channel_id=1, source_target_pairs={{0,16},{16,0},{32,48},{48,32},{64,80},{80,64},{96,112},{112,96},{1... | collective-permute-start | bytes 3145736 | tf_op jit(solution)/shard_map/ppermute | solution.py:33
  70.9 11.5 %collective-permute-start.10 = (bf16[2,4,64,768]{3,2,1,0:T(8,128)(2,1)}, bf16[2,4,64,768]{3,2,1,0:T(8,128)(2,1)}, u32[]{:S(2)}, u32[]{:S(2)}) collective-permute-start(bf16[2,4,64,768]{3,2,1,0:T(8,128)(2,1)} %pad_maximum_fusion.1), channel_id=1, source_target_pairs={{0,3},{1,2},{2,1},{3,0},{4,7},{5,6},{6,5},{7,4},{8,11},{9,10},{10,... | collective-permute-start | bytes 2359304 | tf_op jit(solution)/shard_map/ppermute | solution.py:44
  76.0 1.3 copy-start.18
  84.4 1.2 copy-start.8
  88.6 8.1 %collective-permute-start.11 = (bf16[512,1024]{1,0:T(8,128)(2,1)}, bf16[512,1024]{1,0:T(8,128)(2,1)}, u32[]{:S(2)}, u32[]{:S(2)}) collective-permute-start(bf16[512,1024]{1,0:T(8,128)(2,1)} %convolution_convert_fusion), channel_id=1, source_target_pairs={{0,16},{16,0},{32,48},{48,32},{64,80},{80,64},{96,112},{112,96},{1... | collective-permute-start | bytes 3145736 | tf_op jit(solution)/shard_map/ppermute | solution.py:33
  90.9 25.1 %collective-permute-start.14 = (bf16[2,64,1024]{2,1,0:T(8,128)(2,1)}, bf16[2,64,1024]{2,1,0:T(8,128)(2,1)S(1)}, u32[]{:S(2)}, u32[]{:S(2)}) collective-permute-start(bf16[2,64,1024]{2,1,0:T(8,128)(2,1)} %get-tuple-element.60), channel_id=1, source_target_pairs={{0,128},{16,144},{32,160},{48,176},{64,192},{80,208},{96,224},{112... | collective-permute-start | bytes 786440 | tf_op jit(solution)/shard_map/ppermute | solution.py:33
  91.0 25.0 %collective-permute-start.12 = (bf16[2,64,1024]{2,1,0:T(8,128)(2,1)}, bf16[2,64,1024]{2,1,0:T(8,128)(2,1)S(1)}, u32[]{:S(2)}, u32[]{:S(2)}) collective-permute-start(bf16[2,64,1024]{2,1,0:T(8,128)(2,1)} %get-tuple-element.61), channel_id=1, source_target_pairs={{0,64},{16,80},{32,96},{48,112},{64,128},{80,144},{96,160},{112,17... | collective-permute-start | bytes 786440 | tf_op jit(solution)/shard_map/ppermute | solution.py:33
  94.5 21.6 %collective-permute-start.13 = (bf16[2,64,1024]{2,1,0:T(8,128)(2,1)}, bf16[2,64,1024]{2,1,0:T(8,128)(2,1)S(1)}, u32[]{:S(2)}, u32[]{:S(2)}) collective-permute-start(bf16[2,64,1024]{2,1,0:T(8,128)(2,1)} %get-tuple-element.62), channel_id=1, source_target_pairs={{0,192},{16,208},{32,224},{48,240},{64,0},{80,16},{96,32},{112,48}... | collective-permute-start | bytes 786440 | tf_op jit(solution)/shard_map/ppermute | solution.py:33
  94.5 18.2 %collective-permute-start.20 = (bf16[2,128,768]{2,1,0:T(8,128)(2,1)S(1)}, bf16[2,128,768]{2,1,0:T(8,128)(2,1)S(1)}, u32[]{:S(2)}, u32[]{:S(2)}) collective-permute-start(bf16[2,128,768]{2,1,0:T(8,128)(2,1)S(1)} %bitcast_dynamic-update-slice_fusion.9), channel_id=1, source_target_pairs={{0,12},{1,13},{2,14},{3,15},{4,8},{5,9},{6,10},{7,11},{8,4},{9,5},... | collective-permute-start | bytes 1179656 | tf_op jit(solution)/shard_map/ppermute | solution.py:37
  99.3 17.0 %copy-start.19 = (f32[512,1024]{1,0:T(8,128)}, f32[512,1024]{1,0:T(8,128)S(1)}, u32[]{:S(2)}) copy-start(f32[512,1024]{1,0:T(8,128)S(1)} %convert_add_fusion.1) | copy-start | bytes 6291460
  112.7 14.9 %copy-start.6 = (bf16[2,2,128,768]{3,2,1,0:T(8,128)(2,1)}, bf16[2,2,128,768]{3,2,1,0:T(8,128)(2,1)S(1)}, u32[]{:S(2)}) copy-start(bf16[2,2,128,768]{3,2,1,0:T(8,128)(2,1)S(1)} %bitcast_dynamic-update-slice_fusion.2) | copy-start | bytes 2359300
  112.7 14.9 %collective-permute-start.21 = (bf16[4,128,768]{2,1,0:T(8,128)(2,1)S(1)}, bf16[4,128,768]{2,1,0:T(8,128)(2,1)S(1)}, u32[]{:S(2)}, u32[]{:S(2)}) collective-permute-start(bf16[4,128,768]{2,1,0:T(8,128)(2,1)S(1)} %bitcast.203), channel_id=1, source_target_pairs={{0,1},{1,0},{2,3},{3,2},{4,5},{5,4},{6,7},{7,6},{8,9},{9,8},{10,11... | collective-permute-start | bytes 2359304 | tf_op jit(solution)/shard_map/ppermute | solution.py:44
  116.2 10.1 %collective-permute-start.15 = (bf16[2,64,1024]{2,1,0:T(8,128)(2,1)S(1)}, bf16[2,64,1024]{2,1,0:T(8,128)(2,1)}, u32[]{:S(2)}, u32[]{:S(2)}) collective-permute-start(bf16[2,64,1024]{2,1,0:T(8,128)(2,1)S(1)} %convert_add_fusion.7), channel_id=1, source_target_pairs={{0,32},{16,48},{32,0},{48,16},{64,96},{80,112},{96,64},{112,80},{1... | collective-permute-start | bytes 786440 | tf_op jit(solution)/shard_map/ppermute | solution.py:33
  120.2 15.2 %collective-permute-start.16 = (bf16[2,64,1024]{2,1,0:T(8,128)(2,1)}, bf16[2,64,1024]{2,1,0:T(8,128)(2,1)S(1)}, u32[]{:S(2)}, u32[]{:S(2)}) collective-permute-start(bf16[2,64,1024]{2,1,0:T(8,128)(2,1)} %get-tuple-element.33), channel_id=1, source_target_pairs={{0,64},{16,80},{32,96},{48,112},{64,128},{80,144},{96,160},{112,17... | collective-permute-start | bytes 786440 | tf_op jit(solution)/shard_map/ppermute | solution.py:33
  121.6 13.7 %collective-permute-start.17 = (bf16[2,64,1024]{2,1,0:T(8,128)(2,1)}, bf16[2,64,1024]{2,1,0:T(8,128)(2,1)S(1)}, u32[]{:S(2)}, u32[]{:S(2)}) collective-permute-start(bf16[2,64,1024]{2,1,0:T(8,128)(2,1)} %get-tuple-element.34), channel_id=1, source_target_pairs={{0,192},{16,208},{32,224},{48,240},{64,0},{80,16},{96,32},{112,48}... | collective-permute-start | bytes 786440 | tf_op jit(solution)/shard_map/ppermute | solution.py:33
  122.9 12.5 %collective-permute-start.18 = (bf16[2,64,1024]{2,1,0:T(8,128)(2,1)}, bf16[2,64,1024]{2,1,0:T(8,128)(2,1)S(1)}, u32[]{:S(2)}, u32[]{:S(2)}) collective-permute-start(bf16[2,64,1024]{2,1,0:T(8,128)(2,1)} %get-tuple-element.35), channel_id=1, source_target_pairs={{0,128},{16,144},{32,160},{48,176},{64,192},{80,208},{96,224},{112... | collective-permute-start | bytes 786440 | tf_op jit(solution)/shard_map/ppermute | solution.py:33
  127.6 8.0 %copy-start.11 = (bf16[4,128,768]{2,1,0:T(8,128)(2,1)}, bf16[4,128,768]{2,1,0:T(8,128)(2,1)S(1)}, u32[]{:S(2)}) copy-start(bf16[4,128,768]{2,1,0:T(8,128)(2,1)S(1)} %collective-permute-done.21) | copy-start | bytes 2359300
  127.6 10.9 %copy-start.2 = (bf16[2048,1024]{1,0:T(8,128)(2,1)S(1)}, bf16[2048,1024]{1,0:T(8,128)(2,1)}, u32[]{:S(2)}) copy-start(bf16[2048,1024]{1,0:T(8,128)(2,1)} %all-gather.2.cloned.1.call-done) | copy-start | bytes 12582916
  127.7 30.8 %collective-permute-start.22 = (bf16[2,4,128,768]{3,2,1,0:T(8,128)(2,1)S(1)}, bf16[2,4,128,768]{3,2,1,0:T(8,128)(2,1)S(1)}, u32[]{:S(2)}, u32[]{:S(2)}) collective-permute-start(bf16[2,4,128,768]{3,2,1,0:T(8,128)(2,1)S(1)} %pad_maximum_fusion), channel_id=1, source_target_pairs={{0,3},{1,2},{2,1},{3,0},{4,7},{5,6},{6,5},{7,4},{8,11},{9,10},{10,... | collective-permute-start | bytes 4718600 | tf_op jit(solution)/shard_map/ppermute | solution.py:44
  135.6 21.6 %collective-permute-start.19 = (bf16[2,64,1024]{2,1,0:T(8,128)(2,1)S(1)}, bf16[2,64,1024]{2,1,0:T(8,128)(2,1)S(1)}, u32[]{:S(2)}, u32[]{:S(2)}) collective-permute-start(bf16[2,64,1024]{2,1,0:T(8,128)(2,1)S(1)} %convert_add_fusion.6), channel_id=1, source_target_pairs={{0,32},{16,48},{32,0},{48,16},{64,96},{80,112},{96,64},{112,80},{1... | collective-permute-start | bytes 786440 | tf_op jit(solution)/shard_map/ppermute | solution.py:33
  135.7 7.0 %collective-permute-start.23 = (bf16[2,64,1024]{2,1,0:T(8,128)(2,1)S(1)}, bf16[2,64,1024]{2,1,0:T(8,128)(2,1)S(1)}, u32[]{:S(2)}, u32[]{:S(2)}) collective-permute-start(bf16[2,64,1024]{2,1,0:T(8,128)(2,1)S(1)} %fusion.26), channel_id=1, source_target_pairs={{0,64},{16,208},{32,96},{48,240},{64,0},{80,144},{96,32},{112,176}... | collective-permute-start | bytes 786440 | tf_op jit(solution)/shard_map/ppermute | solution.py:51
  139.0 18.2 %copy-start.10 = (f32[2,128,1024]{2,1,0:T(8,128)S(1)}, f32[2,128,1024]{2,1,0:T(8,128)}, u32[]{:S(2)}) copy-start(f32[2,128,1024]{2,1,0:T(8,128)} %fusion.18) | copy-start | bytes 3145732
  142.6 14.7 %copy-start.7 = (bf16[2,2,128,768]{3,2,1,0:T(8,128)(2,1)S(1)}, bf16[2,2,128,768]{3,2,1,0:T(8,128)(2,1)}, u32[]{:S(2)}) copy-start(bf16[2,2,128,768]{3,2,1,0:T(8,128)(2,1)} %copy-done.6) | copy-start | bytes 2359300
  142.7 22.8 %collective-permute-start.24 = (bf16[2,2,64,1024]{3,2,1,0:T(8,128)(2,1)S(1)}, bf16[2,2,64,1024]{3,2,1,0:T(8,128)(2,1)S(1)}, u32[]{:S(2)}, u32[]{:S(2)}) collective-permute-start(bf16[2,2,64,1024]{3,2,1,0:T(8,128)(2,1)S(1)} %pad_maximum_fusion.2), channel_id=1, source_target_pairs={{0,192},{16,80},{32,224},{48,112},{64,128},{80,16},{96,160},{112,4... | collective-permute-start | bytes 1572872 | tf_op jit(solution)/shard_map/ppermute | solution.py:51
  167.0 9.8 %collective-permute-start.25 = (bf16[2,4,64,1024]{3,2,1,0:T(8,128)(2,1)}, bf16[2,4,64,1024]{3,2,1,0:T(8,128)(2,1)}, u32[]{:S(2)}, u32[]{:S(2)}) collective-permute-start(bf16[2,4,64,1024]{3,2,1,0:T(8,128)(2,1)} %fusion.41), channel_id=1, source_target_pairs={{0,16},{16,0},{32,48},{48,32},{64,80},{80,64},{96,112},{112,96},{1... | collective-permute-start | bytes 3145736 | tf_op jit(solution)/shard_map/ppermute | solution.py:33
  168.8 6.8 %collective-permute-start.26 = (bf16[2,64,1024]{2,1,0:T(8,128)(2,1)S(1)}, bf16[2,64,1024]{2,1,0:T(8,128)(2,1)}, u32[]{:S(2)}, u32[]{:S(2)}) collective-permute-start(bf16[2,64,1024]{2,1,0:T(8,128)(2,1)S(1)} %fusion.25), channel_id=1, source_target_pairs={{0,64},{16,208},{32,96},{48,240},{64,0},{80,144},{96,32},{112,176}... | collective-permute-start | bytes 786440 | tf_op jit(solution)/shard_map/ppermute | solution.py:51
  176.6 3.0 %copy-start.22 = (bf16[768,1024]{1,0:T(8,128)(2,1)S(1)}, bf16[768,1024]{1,0:T(8,128)(2,1)}, u32[]{:S(2)}) copy-start(bf16[768,1024]{1,0:T(8,128)(2,1)} %param.8) | copy-start | bytes 4718596
  176.7 8.9 %collective-permute-start.27 = (bf16[2,2,64,1024]{3,2,1,0:T(8,128)(2,1)S(1)}, bf16[2,2,64,1024]{3,2,1,0:T(8,128)(2,1)S(1)}, u32[]{:S(2)}, u32[]{:S(2)}) collective-permute-start(bf16[2,2,64,1024]{3,2,1,0:T(8,128)(2,1)S(1)} %pad_maximum_fusion.3), channel_id=1, source_target_pairs={{0,192},{16,80},{32,224},{48,112},{64,128},{80,16},{96,160},{112,4... | collective-permute-start | bytes 1572872 | tf_op jit(solution)/shard_map/ppermute | solution.py:51
  179.7 1.9 copy-start.4
  181.5 4.1 %copy-start.16 = (f32[4,4,64,768]{3,2,1,0:T(8,128)}, f32[4,4,64,768]{3,2,1,0:T(8,128)S(1)}, u32[]{:S(2)}) copy-start(f32[4,4,64,768]{3,2,1,0:T(8,128)S(1)} %fusion.11) | copy-start | bytes 9437188
  187.1 5.4 %collective-permute-start.28 = (bf16[2,4,64,1024]{3,2,1,0:T(8,128)(2,1)}, bf16[2,4,64,1024]{3,2,1,0:T(8,128)(2,1)}, u32[]{:S(2)}, u32[]{:S(2)}) collective-permute-start(bf16[2,4,64,1024]{3,2,1,0:T(8,128)(2,1)} %fusion.39), channel_id=1, source_target_pairs={{0,16},{16,0},{32,48},{48,32},{64,80},{80,64},{96,112},{112,96},{1... | collective-permute-start | bytes 3145736 | tf_op jit(solution)/shard_map/ppermute | solution.py:33
  189.9 5.4 %copy-start.23 = (bf16[768,1024]{1,0:T(8,128)(2,1)S(1)}, bf16[768,1024]{1,0:T(8,128)(2,1)}, u32[]{:S(2)}) copy-start(bf16[768,1024]{1,0:T(8,128)(2,1)} %param.8) | copy-start | bytes 4718596
  189.9 19.2 %collective-permute-start.31 = (bf16[4,64,768]{2,1,0:T(8,128)(2,1)}, bf16[4,64,768]{2,1,0:T(8,128)(2,1)S(1)}, u32[]{:S(2)}, u32[]{:S(2)}) collective-permute-start(bf16[4,64,768]{2,1,0:T(8,128)(2,1)} %get-tuple-element.54), channel_id=1, source_target_pairs={{0,2},{1,3},{2,0},{3,1},{4,6},{5,7},{6,4},{7,5},{8,10},{9,11},{10,... | collective-permute-start | bytes 1179656 | tf_op jit(solution)/shard_map/ppermute | solution.py:33
  190.0 19.5 %collective-permute-start.30 = (bf16[4,64,768]{2,1,0:T(8,128)(2,1)}, bf16[4,64,768]{2,1,0:T(8,128)(2,1)S(1)}, u32[]{:S(2)}, u32[]{:S(2)}) collective-permute-start(bf16[4,64,768]{2,1,0:T(8,128)(2,1)} %get-tuple-element.55), channel_id=1, source_target_pairs={{0,3},{1,0},{2,1},{3,2},{4,7},{5,4},{6,5},{7,6},{8,11},{9,8},{10,9... | collective-permute-start | bytes 1179656 | tf_op jit(solution)/shard_map/ppermute | solution.py:33
  191.5 19.6 %collective-permute-start.29 = (bf16[4,64,768]{2,1,0:T(8,128)(2,1)}, bf16[4,64,768]{2,1,0:T(8,128)(2,1)S(1)}, u32[]{:S(2)}, u32[]{:S(2)}) collective-permute-start(bf16[4,64,768]{2,1,0:T(8,128)(2,1)} %get-tuple-element.56), channel_id=1, source_target_pairs={{0,1},{1,2},{2,3},{3,0},{4,5},{5,6},{6,7},{7,4},{8,9},{9,10},{10,1... | collective-permute-start | bytes 1179656 | tf_op jit(solution)/shard_map/ppermute | solution.py:33
  197.1 2.4 copy-start.3
  199.6 1.4 copy-start.9
  199.6 2.4 copy-start.24
  205.6 1.6 copy-start.5
  211.3 29.8 %collective-permute-start.34 = (bf16[64,768]{1,0:T(8,128)(2,1)S(1)}, bf16[64,768]{1,0:T(8,128)(2,1)S(1)}, u32[]{:S(2)}, u32[]{:S(2)}) collective-permute-start(bf16[64,768]{1,0:T(8,128)(2,1)S(1)} %get-tuple-element.70), channel_id=1, source_target_pairs={{0,8},{1,9},{2,10},{3,11},{4,12},{5,13},{6,14},{7,15},{8,0},{9,1},... | collective-permute-start | bytes 294920 | tf_op jit(solution)/shard_map/ppermute | solution.py:33
  213.7 30.7 %collective-permute-start.33 = (bf16[64,768]{1,0:T(8,128)(2,1)S(1)}, bf16[64,768]{1,0:T(8,128)(2,1)S(1)}, u32[]{:S(2)}, u32[]{:S(2)}) collective-permute-start(bf16[64,768]{1,0:T(8,128)(2,1)S(1)} %get-tuple-element.71), channel_id=1, source_target_pairs={{0,12},{1,13},{2,14},{3,15},{4,0},{5,1},{6,2},{7,3},{8,4},{9,5},{1... | collective-permute-start | bytes 294920 | tf_op jit(solution)/shard_map/ppermute | solution.py:33
  215.3 9.6 %collective-permute-start.36 = (bf16[4,64,768]{2,1,0:T(8,128)(2,1)S(1)}, bf16[4,64,768]{2,1,0:T(8,128)(2,1)S(1)}, u32[]{:S(2)}, u32[]{:S(2)}) collective-permute-start(bf16[4,64,768]{2,1,0:T(8,128)(2,1)S(1)} %get-tuple-element.49), channel_id=1, source_target_pairs={{0,3},{1,0},{2,1},{3,2},{4,7},{5,4},{6,5},{7,6},{8,11},{9,8},{10,9... | collective-permute-start | bytes 1179656 | tf_op jit(solution)/shard_map/ppermute | solution.py:33
  216.5 10.9 %collective-permute-start.37 = (bf16[4,64,768]{2,1,0:T(8,128)(2,1)S(1)}, bf16[4,64,768]{2,1,0:T(8,128)(2,1)S(1)}, u32[]{:S(2)}, u32[]{:S(2)}) collective-permute-start(bf16[4,64,768]{2,1,0:T(8,128)(2,1)S(1)} %get-tuple-element.50), channel_id=1, source_target_pairs={{0,2},{1,3},{2,0},{3,1},{4,6},{5,7},{6,4},{7,5},{8,10},{9,11},{10,... | collective-permute-start | bytes 1179656 | tf_op jit(solution)/shard_map/ppermute | solution.py:33
  216.5 20.4 %collective-permute-start.35 = (bf16[4,64,768]{2,1,0:T(8,128)(2,1)S(1)}, bf16[4,64,768]{2,1,0:T(8,128)(2,1)S(1)}, u32[]{:S(2)}, u32[]{:S(2)}) collective-permute-start(bf16[4,64,768]{2,1,0:T(8,128)(2,1)S(1)} %get-tuple-element.48), channel_id=1, source_target_pairs={{0,1},{1,2},{2,3},{3,0},{4,5},{5,6},{6,7},{7,4},{8,9},{9,10},{10,1... | collective-permute-start | bytes 1179656 | tf_op jit(solution)/shard_map/ppermute | solution.py:33
  220.8 32.8 %copy-start.1 = (bf16[1024,768]{1,0:T(8,128)(2,1)S(1)}, bf16[1024,768]{1,0:T(8,128)(2,1)}, u32[]{:S(2)}) copy-start(bf16[1024,768]{1,0:T(8,128)(2,1)} %param.9) | copy-start | bytes 4718596
  224.9 19.4 %collective-permute-start.32 = (bf16[64,768]{1,0:T(8,128)(2,1)S(1)}, bf16[64,768]{1,0:T(8,128)(2,1)S(1)}, u32[]{:S(2)}, u32[]{:S(2)}) collective-permute-start(bf16[64,768]{1,0:T(8,128)(2,1)S(1)} %get-tuple-element.72), channel_id=1, source_target_pairs={{0,4},{1,5},{2,6},{3,7},{4,8},{5,9},{6,10},{7,11},{8,12},{9,13},{1... | collective-permute-start | bytes 294920 | tf_op jit(solution)/shard_map/ppermute | solution.py:33
  237.1 7.3 %collective-permute-start.38 = (bf16[64,768]{1,0:T(8,128)(2,1)S(1)}, bf16[64,768]{1,0:T(8,128)(2,1)S(1)}, u32[]{:S(2)}, u32[]{:S(2)}) collective-permute-start(bf16[64,768]{1,0:T(8,128)(2,1)S(1)} %get-tuple-element.67), channel_id=1, source_target_pairs={{0,4},{1,5},{2,6},{3,7},{4,8},{5,9},{6,10},{7,11},{8,12},{9,13},{1... | collective-permute-start | bytes 294920 | tf_op jit(solution)/shard_map/ppermute | solution.py:33
  238.9 9.3 %collective-permute-start.40 = (bf16[64,768]{1,0:T(8,128)(2,1)S(1)}, bf16[64,768]{1,0:T(8,128)(2,1)S(1)}, u32[]{:S(2)}, u32[]{:S(2)}) collective-permute-start(bf16[64,768]{1,0:T(8,128)(2,1)S(1)} %get-tuple-element.68), channel_id=1, source_target_pairs={{0,8},{1,9},{2,10},{3,11},{4,12},{5,13},{6,14},{7,15},{8,0},{9,1},... | collective-permute-start | bytes 294920 | tf_op jit(solution)/shard_map/ppermute | solution.py:33
  241.1 11.7 %collective-permute-start.39 = (bf16[64,768]{1,0:T(8,128)(2,1)S(1)}, bf16[64,768]{1,0:T(8,128)(2,1)S(1)}, u32[]{:S(2)}, u32[]{:S(2)}) collective-permute-start(bf16[64,768]{1,0:T(8,128)(2,1)S(1)} %get-tuple-element.69), channel_id=1, source_target_pairs={{0,12},{1,13},{2,14},{3,15},{4,0},{5,1},{6,2},{7,3},{8,4},{9,5},{1... | collective-permute-start | bytes 294920 | tf_op jit(solution)/shard_map/ppermute | solution.py:33
  (3 other events, 3.1 us)
Sparse Core Ops, SparseCore 0:
  9.9 61.7 all-gather.1
where the time goes:
time: 263 us; the launch traced here: 261 us
  waiting for transfers between devices  90.5 us (34%)
  starting transfers between devices  84.1 us (32%)
  local copies, waits for them, and re-layouts  37.3 us (14%)
  matrix products  25.3 us (10%)
  between operations  14.9 us (6%)
  other arithmetic  8.5 us (3%)
    ppermute x31, waiting for transfers between devices, move(): return lax.ppermute(v, axis, [(i, to(i)) for i in range(16)])  63 us
    ppermute x31, starting transfers between devices, move(): return lax.ppermute(v, axis, [(i, to(i)) for i in range(16)])  51.5 us
    ppermute x4, starting transfers between devices, around_y(): return lax.ppermute(v, 'row', [(i, to(i)) for i in range(16)])  20.3 us
    dot_general x4, matrix products, token_contract(): lax.dot_general(left, right, (((0,), (0,)), ((), ())), preferred_element_...  12.7 us
    dot_general x6, matrix products, width_contract(): lax.dot_general(left, right, (((1,), (1,)), ((), ())), preferred_element_...  12.6 us
    ppermute x2, waiting for transfers between devices, swap(): return lax.ppermute(v, axis, [(i, i ^ bit) for i in range(16)])  12.3 us
    dynamic_update_slice x23, local copies, waits for them, and re-layouts, put(): lax.dynamic_update_slice_in_dim(whole, jnp.expand_dims(piece, dim), at, dim)  10.4 us
    ppermute x4, waiting for transfers between devices, around_y(): return lax.ppermute(v, 'row', [(i, to(i)) for i in range(16)])  8.87 us
  transfers between devices with their start and end apart: 42, of which 19 were waited for; matrix products, arithmetic and copies ran while one was open for 20% of the time, Pallas kernels for 0%

commit v1 on v0

--- a/solution.py
+++ b/solution.py
@@ -181,13 +181,13 @@
 
     mine1 = core_sum(og1)
     away1 = blocks_away(mine1, y, 1)
-    input_z = pair2(low, swap(after(low, og1), "col", 12), zh // 2, 0, hold=tuple(away1))
+    pair0 = scatter4(along_y, mine0, away0, y, 1, hold=tuple(away1))
+    gpre0 = pre_grad(pair0.astype(BF), 0)
+    input_z = pair2(low, swap(after(low, og1), "col", 12), zh // 2, 0, hold=(gpre0,))
     input_z = input_z.reshape(4, tokens, width)
     input_near = around_x(input_z, True)
     input_far = around_x(jnp.stack([input_z, input_near]), False)
     input_panel = place4(input_z, input_near, input_far, x, core, 0)
-    pair0 = scatter4(along_y, mine0, away0, y, 1, hold=tuple(away1))
-    gpre0 = pre_grad(pair0.astype(BF), 0)
     pair1 = scatter4(along_y, mine1, [after(v, pair0) for v in away1], y, 1, hold=(gpre0,))
     sent1 = pair1.astype(BF)
     weight_out_grad = out_term(0, og0, sent1)

time: 263 us -> 275 us (1.046)
  waiting for transfers between devices: 90.5 us -> 99.4 us
  local copies, waits for them, and re-layouts: 37.3 us -> 40.9 us
    ppermute x31, waiting for transfers between devices: 63 us -> 72 us  [move(): return lax.ppermute(v, axis, [(i, to(i)) for i in range(16)])]
    broadcast_in_dim x11, local copies, waits for them, and re-layouts: 8.12 us -> 11.8 us  [spread(): return jnp.broadcast_to(jnp.expand_dims(own, dim), shape)]
    unnamed x50 -> x44, local copies, waits for them, and re-layouts: 8.23 us -> 6.18 us
  transfers between devices with their start and end apart: 42 -> 42, of which waited for: 19 -> 23; matrix products, arithmetic and copies ran while one was open for 20% -> 21% of each run, Pallas kernels for 0% -> 0%
where the time goes in v1:
time: 275 us; the launch traced here: 273 us
  waiting for transfers between devices  99.4 us (36%)
  starting transfers between devices  82.9 us (30%)
  local copies, waits for them, and re-layouts  40.9 us (15%)
  matrix products  26.6 us (10%)
  between operations  14.8 us (5%)
  other arithmetic  8.04 us (3%)
    ppermute x31, waiting for transfers between devices, move(): return lax.ppermute(v, axis, [(i, to(i)) for i in range(16)])  72 us
    ppermute x31, starting transfers between devices, move(): return lax.ppermute(v, axis, [(i, to(i)) for i in range(16)])  50.9 us
    ppermute x4, starting transfers between devices, around_y(): return lax.ppermute(v, 'row', [(i, to(i)) for i in range(16)])  18.1 us
    dot_general x6, matrix products, width_contract(): lax.dot_general(left, right, (((1,), (1,)), ((), ())), preferred_element_...  13.9 us
    dot_general x4, matrix products, token_contract(): lax.dot_general(left, right, (((0,), (0,)), ((), ())), preferred_element_...  12.7 us
    broadcast_in_dim x11, local copies, waits for them, and re-layouts, spread(): return jnp.broadcast_to(jnp.expand_dims(own, dim), shape)  11.8 us
    dynamic_update_slice x23, local copies, waits for them, and re-layouts, put(): lax.dynamic_update_slice_in_dim(whole, jnp.expand_dims(piece, dim), at, dim)  11.1 us
    ppermute x4, waiting for transfers between devices, around_y(): return lax.ppermute(v, 'row', [(i, to(i)) for i in range(16)])  10 us
  transfers between devices with their start and end apart: 42, of which 23 were waited for; matrix products, arithmetic and copies ran while one was open for 21% of the time, Pallas kernels for 0%

profile of v1, /device:TPU:1, one launch (start us, length us, event | category | flops | bytes accessed | tf_op | source)
XLA Modules:
  0.0 272.7 jit_solution(9035204142188425749)
XLA Ops:
  7.2 1.9 fusion.21
  9.2 3.9 %collective-permute-start = (bf16[128,768]{1,0:T(8,128)(2,1)}, bf16[128,768]{1,0:T(8,128)(2,1)S(1)}, u32[]{:S(2)}, u32[]{:S(2)}) collective-permute-start(bf16[128,768]{1,0:T(8,128)(2,1)} %param.6), channel_id=1, source_target_pairs={{0,4},{1,5},{2,6},{3,7},{4,8},{5,9},{6,10},{7,11},{8,12},{9,13},{1... | collective-permute-start | bytes 589832 | tf_op jit(solution)/shard_map/ppermute | solution.py:33
  13.1 5.1 %collective-permute-start.2 = (bf16[128,768]{1,0:T(8,128)(2,1)}, bf16[128,768]{1,0:T(8,128)(2,1)S(1)}, u32[]{:S(2)}, u32[]{:S(2)}) collective-permute-start(bf16[128,768]{1,0:T(8,128)(2,1)} %param.6), channel_id=1, source_target_pairs={{0,8},{1,9},{2,10},{3,11},{4,12},{5,13},{6,14},{7,15},{8,0},{9,1},... | collective-permute-start | bytes 589832 | tf_op jit(solution)/shard_map/ppermute | solution.py:33
  18.2 2.4 collective-permute-start.1
  22.6 12.0 %collective-permute-done.1 = bf16[128,768]{1,0:T(8,128)(2,1)S(1)} collective-permute-done((bf16[128,768]{1,0:T(8,128)(2,1)}, bf16[128,768]{1,0:T(8,128)(2,1)S(1)}, u32[]{:S(2)}, u32[]{:S(2)}) %collective-permute-start.1) | collective-permute-done | bytes 196640 | tf_op jit(solution)/shard_map/ppermute | solution.py:33
  34.7 2.8 %collective-permute-start.8 = (bf16[4,64,768]{2,1,0:T(8,128)(2,1)S(1)}, bf16[4,64,768]{2,1,0:T(8,128)(2,1)S(1)}, u32[]{:S(2)}, u32[]{:S(2)}) collective-permute-start(bf16[4,64,768]{2,1,0:T(8,128)(2,1)S(1)} %get-tuple-element.75), channel_id=1, source_target_pairs={{0,2},{1,3},{2,0},{3,1},{4,6},{5,7},{6,4},{7,5},{8,10},{9,11},{10,... | collective-permute-start | bytes 1179656 | tf_op jit(solution)/shard_map/ppermute | solution.py:33
  38.9 3.8 %collective-permute-start.4 = (bf16[128,768]{1,0:T(8,128)(2,1)}, bf16[128,768]{1,0:T(8,128)(2,1)S(1)}, u32[]{:S(2)}, u32[]{:S(2)}) collective-permute-start(bf16[128,768]{1,0:T(8,128)(2,1)} %param.5), channel_id=1, source_target_pairs={{0,4},{1,5},{2,6},{3,7},{4,0},{5,1},{6,2},{7,3},{8,12},{9,13},{10,... | collective-permute-start | bytes 589832 | tf_op jit(solution)/shard_map/ppermute | solution.py:37
  42.7 13.6 %collective-permute-done.3 = bf16[128,1024]{1,0:T(8,128)(2,1)S(1)} collective-permute-done((bf16[128,1024]{1,0:T(8,128)(2,1)}, bf16[128,1024]{1,0:T(8,128)(2,1)S(1)}, u32[]{:S(2)}, u32[]{:S(2)}) %collective-permute-start.3) | collective-permute-done | bytes 262176 | tf_op jit(solution)/shard_map/ppermute | solution.py:33
  56.3 2.5 collective-permute-start.5
  58.9 1.6 fusion.18
  60.6 1.7 broadcast_in_dim.117
  66.4 2.0 convolution_convert_fusion.1
  68.4 1.7 collective-permute-start.9
  70.1 1.2 collective-permute-start.10
  71.4 1.4 collective-permute-done.9
  72.8 3.8 %convert_add_fusion.2 = f32[512,1024]{1,0:T(8,128)} fusion(bf16[512,1024]{1,0:T(8,128)(2,1)} %collective-permute-done.9, bf16[512,768]{1,0:T(8,128)(2,1)} %bitcast.221, bf16[1024,768]{1,0:T(8,128)(2,1)S(1)} %copy-done), kind=kOutput, calls=%fused_computation.15 | convolution fusion | flops 806354944 | bytes 5505024 | tf_op jit(solution)/shard_map/dot_general | solution.py:25
  76.6 2.3 fusion.33
  80.1 1.5 collective-permute-done.10
  83.7 1.2 copy-done.8
  85.9 2.0 convolution_convert_fusion
  87.9 2.3 collective-permute-start.11
  90.4 3.4 %collective-permute-start.12 = (bf16[2,64,1024]{2,1,0:T(8,128)(2,1)}, bf16[2,64,1024]{2,1,0:T(8,128)(2,1)S(1)}, u32[]{:S(2)}, u32[]{:S(2)}) collective-permute-start(bf16[2,64,1024]{2,1,0:T(8,128)(2,1)} %get-tuple-element.61), channel_id=1, source_target_pairs={{0,64},{16,80},{32,96},{48,112},{64,128},{80,144},{96,160},{112,17... | collective-permute-start | bytes 786440 | tf_op jit(solution)/shard_map/ppermute | solution.py:33
  94.9 2.5 convert_add_fusion.1
  98.3 1.6 collective-permute-done.14
  99.9 5.8 %collective-permute-done.12 = bf16[2,64,1024]{2,1,0:T(8,128)(2,1)S(1)} collective-permute-done((bf16[2,64,1024]{2,1,0:T(8,128)(2,1)}, bf16[2,64,1024]{2,1,0:T(8,128)(2,1)S(1)}, u32[]{:S(2)}, u32[]{:S(2)}) %collective-permute-start.12) | collective-permute-done | bytes 262176 | tf_op jit(solution)/shard_map/ppermute | solution.py:33
  106.7 4.2 %collective-permute-start.20 = (bf16[2,128,768]{2,1,0:T(8,128)(2,1)}, bf16[2,128,768]{2,1,0:T(8,128)(2,1)}, u32[]{:S(2)}, u32[]{:S(2)}) collective-permute-start(bf16[2,128,768]{2,1,0:T(8,128)(2,1)} %bitcast_dynamic-update-slice_fusion.9), channel_id=1, source_target_pairs={{0,12},{1,13},{2,14},{3,15},{4,8},{5,9},{6,10},{7,11},{8,4},{9,5},... | collective-permute-start | bytes 1179656 | tf_op jit(solution)/shard_map/ppermute | solution.py:37
  110.9 5.6 %collective-permute-done.15 = bf16[2,64,1024]{2,1,0:T(8,128)(2,1)S(1)} collective-permute-done((bf16[2,64,1024]{2,1,0:T(8,128)(2,1)S(1)}, bf16[2,64,1024]{2,1,0:T(8,128)(2,1)S(1)}, u32[]{:S(2)}, u32[]{:S(2)}) %collective-permute-start.15) | collective-permute-done | bytes 262176 | tf_op jit(solution)/shard_map/ppermute | solution.py:33
  117.6 9.8 %collective-permute-done.20 = bf16[2,128,768]{2,1,0:T(8,128)(2,1)} collective-permute-done((bf16[2,128,768]{2,1,0:T(8,128)(2,1)}, bf16[2,128,768]{2,1,0:T(8,128)(2,1)}, u32[]{:S(2)}, u32[]{:S(2)}) %collective-permute-start.20) | collective-permute-done | bytes 393248 | tf_op jit(solution)/shard_map/ppermute | solution.py:37
  128.4 2.1 collective-permute-start.21
  130.9 2.4 collective-permute-start.17
  133.3 1.2 collective-permute-start.18
  135.6 4.9 %collective-permute-done.21 = bf16[4,128,768]{2,1,0:T(8,128)(2,1)S(1)} collective-permute-done((bf16[4,128,768]{2,1,0:T(8,128)(2,1)S(1)}, bf16[4,128,768]{2,1,0:T(8,128)(2,1)S(1)}, u32[]{:S(2)}, u32[]{:S(2)}) %collective-permute-start.21) | collective-permute-done | bytes 786464 | tf_op jit(solution)/shard_map/ppermute | solution.py:44
  140.8 4.2 %collective-permute-done.17 = bf16[2,64,1024]{2,1,0:T(8,128)(2,1)S(1)} collective-permute-done((bf16[2,64,1024]{2,1,0:T(8,128)(2,1)}, bf16[2,64,1024]{2,1,0:T(8,128)(2,1)S(1)}, u32[]{:S(2)}, u32[]{:S(2)}) %collective-permute-start.17) | collective-permute-done | bytes 262176 | tf_op jit(solution)/shard_map/ppermute | solution.py:33
  145.0 2.1 collective-permute-done.18
  147.2 1.6 collective-permute-start.19
  148.8 1.7 collective-permute-start.23
  151.1 3.6 %fusion.4 = f32[1024,768]{1,0:T(8,128)} fusion(bf16[4,4,64,768]{3,2,1,0:T(8,128)(2,1)S(1)} %bitcast_dynamic-update-slice_fusion.3, bf16[4,4,128,1024]{3,2,1,0:T(8,128)(2,1)S(1)} %bitcast.210), kind=kOutput, calls=%fused_computation.16 | convolution fusion | flops 1610612736 | bytes 6815744 | tf_op jit(solution)/shard_map/dot_general | solution.py:21
  155.6 14.5 %collective-permute-start.24 = (bf16[2,2,64,1024]{3,2,1,0:T(8,128)(2,1)S(1)}, bf16[2,2,64,1024]{3,2,1,0:T(8,128)(2,1)S(1)}, u32[]{:S(2)}, u32[]{:S(2)}) collective-permute-start(bf16[2,2,64,1024]{3,2,1,0:T(8,128)(2,1)S(1)} %pad_maximum_fusion.2), channel_id=1, source_target_pairs={{0,192},{16,80},{32,224},{48,112},{64,128},{80,16},{96,160},{112,4... | collective-permute-start | bytes 1572872 | tf_op jit(solution)/shard_map/ppermute | solution.py:51
  174.1 4.3 %collective-permute-done.24 = bf16[2,2,64,1024]{3,2,1,0:T(8,128)(2,1)S(1)} collective-permute-done((bf16[2,2,64,1024]{3,2,1,0:T(8,128)(2,1)S(1)}, bf16[2,2,64,1024]{3,2,1,0:T(8,128)(2,1)S(1)}, u32[]{:S(2)}, u32[]{:S(2)}) %collective-permute-start.24) | collective-permute-done | bytes 524320 | tf_op jit(solution)/shard_map/ppermute | solution.py:51
  179.9 2.4 collective-permute-start.25
  182.2 1.8 collective-permute-start.26
  184.0 4.9 %collective-permute-done.26 = bf16[2,64,1024]{2,1,0:T(8,128)(2,1)S(1)} collective-permute-done((bf16[2,64,1024]{2,1,0:T(8,128)(2,1)}, bf16[2,64,1024]{2,1,0:T(8,128)(2,1)S(1)}, u32[]{:S(2)}, u32[]{:S(2)}) %collective-permute-start.26) | collective-permute-done | bytes 262176 | tf_op jit(solution)/shard_map/ppermute | solution.py:51
  190.0 1.6 broadcast_in_dim.130
  191.6 1.3 bitcast_dynamic-update-slice_fusion.1
  192.9 1.8 fusion.11
  195.9 2.3 broadcast_in_dim.132
  200.4 1.9 collective-permute-start.28
  204.9 1.5 broadcast_in_dim.134
  206.4 1.3 bitcast_dynamic-update-slice_fusion
  207.7 1.8 fusion.9
  209.7 1.5 dynamic-slice_bitcast_fusion
  214.3 3.7 %bitcast_add_fusion = f32[1024,768]{1,0:T(8,128)} fusion(f32[1024,768]{1,0:T(8,128)S(1)} %copy-done.21, bf16[4,4,64,768]{3,2,1,0:T(8,128)(2,1)S(1)} %copy-done.9, bf16[4,4,128,1024]{3,2,1,0:T(8,128)(2,1)S(1)} %bitcast.209), kind=kOutput, calls=%fused_computation.2 | convolution fusion | flops 1611399168 | bytes 9961472 | tf_op jit(solution)/shard_map/dot_general | solution.py:21
  218.1 1.5 copy-done.5
  219.6 1.8 fusion.55
  221.4 2.0 collective-permute-done.29
  223.6 2.6 collective-permute-start.34
  228.0 3.6 %convolution_add_fusion = f32[768,1024]{1,0:T(8,128)} fusion(f32[768,1024]{1,0:T(8,128)S(1)} %fusion.55, bf16[1024,768]{1,0:T(8,128)(2,1)S(1)} %bitcast.215, bf16[1024,1024]{1,0:T(8,128)(2,1)S(1)} %bitcast.214), kind=kOutput, calls=%fused_computation.17 | convolution fusion | flops 1611399168 | bytes 9961472 | tf_op jit(solution)/shard_map/dot_general | solution.py:21
  231.6 4.8 %collective-permute-done.36 = bf16[4,64,768]{2,1,0:T(8,128)(2,1)S(1)} collective-permute-done((bf16[4,64,768]{2,1,0:T(8,128)(2,1)S(1)}, bf16[4,64,768]{2,1,0:T(8,128)(2,1)S(1)}, u32[]{:S(2)}, u32[]{:S(2)}) %collective-permute-start.36) | collective-permute-done | bytes 393248 | tf_op jit(solution)/shard_map/ppermute | solution.py:33
  236.4 1.9 collective-permute-start.32
  238.3 9.8 %collective-permute-done.35 = bf16[4,64,768]{2,1,0:T(8,128)(2,1)S(1)} collective-permute-done((bf16[4,64,768]{2,1,0:T(8,128)(2,1)S(1)}, bf16[4,64,768]{2,1,0:T(8,128)(2,1)S(1)}, u32[]{:S(2)}, u32[]{:S(2)}) %collective-permute-start.35) | collective-permute-done | bytes 393248 | tf_op jit(solution)/shard_map/ppermute | solution.py:33
  248.3 2.4 collective-permute-start.38
  250.7 3.1 %collective-permute-start.40 = (bf16[64,768]{1,0:T(8,128)(2,1)S(1)}, bf16[64,768]{1,0:T(8,128)(2,1)S(1)}, u32[]{:S(2)}, u32[]{:S(2)}) collective-permute-start(bf16[64,768]{1,0:T(8,128)(2,1)S(1)} %get-tuple-element.68), channel_id=1, source_target_pairs={{0,8},{1,9},{2,10},{3,11},{4,12},{5,13},{6,14},{7,15},{8,0},{9,1},... | collective-permute-start | bytes 294920 | tf_op jit(solution)/shard_map/ppermute | solution.py:33
  253.8 3.5 %collective-permute-start.39 = (bf16[64,768]{1,0:T(8,128)(2,1)S(1)}, bf16[64,768]{1,0:T(8,128)(2,1)S(1)}, u32[]{:S(2)}, u32[]{:S(2)}) collective-permute-start(bf16[64,768]{1,0:T(8,128)(2,1)S(1)} %get-tuple-element.69), channel_id=1, source_target_pairs={{0,12},{1,13},{2,14},{3,15},{4,0},{5,1},{6,2},{7,3},{8,4},{9,5},{1... | collective-permute-start | bytes 294920 | tf_op jit(solution)/shard_map/ppermute | solution.py:33
  258.2 6.7 %collective-permute-done.39 = bf16[64,768]{1,0:T(8,128)(2,1)S(1)} collective-permute-done((bf16[64,768]{1,0:T(8,128)(2,1)S(1)}, bf16[64,768]{1,0:T(8,128)(2,1)S(1)}, u32[]{:S(2)}, u32[]{:S(2)}) %collective-permute-start.39) | collective-permute-done | bytes 98336 | tf_op jit(solution)/shard_map/ppermute | solution.py:33
  (140 shorter events, 40.5 us)
Async XLA Ops:
  7.2 59.3 %copy-start = (bf16[1024,768]{1,0:T(8,128)(2,1)S(1)}, bf16[1024,768]{1,0:T(8,128)(2,1)}, u32[]{:S(2)}) copy-start(bf16[1024,768]{1,0:T(8,128)(2,1)} %param.9) | copy-start | bytes 4718596
  7.2 71.7 %all-gather.2.cloned.1.call-start = ((), (), s32[]{:S(2)}) async-start(), calls=%async_computation | async-start | bytes 4456448 | tf_op jit(solution)/shard_map/all_gather | solution.py:163
  9.2 12.4 %collective-permute-start = (bf16[128,768]{1,0:T(8,128)(2,1)}, bf16[128,768]{1,0:T(8,128)(2,1)S(1)}, u32[]{:S(2)}, u32[]{:S(2)}) collective-permute-start(bf16[128,768]{1,0:T(8,128)(2,1)} %param.6), channel_id=1, source_target_pairs={{0,4},{1,5},{2,6},{3,7},{4,8},{5,9},{6,10},{7,11},{8,12},{9,13},{1... | collective-permute-start | bytes 589832 | tf_op jit(solution)/shard_map/ppermute | solution.py:33
  13.1 21.5 %collective-permute-start.2 = (bf16[128,768]{1,0:T(8,128)(2,1)}, bf16[128,768]{1,0:T(8,128)(2,1)S(1)}, u32[]{:S(2)}, u32[]{:S(2)}) collective-permute-start(bf16[128,768]{1,0:T(8,128)(2,1)} %param.6), channel_id=1, source_target_pairs={{0,8},{1,9},{2,10},{3,11},{4,12},{5,13},{6,14},{7,15},{8,0},{9,1},... | collective-permute-start | bytes 589832 | tf_op jit(solution)/shard_map/ppermute | solution.py:33
  18.2 16.3 %collective-permute-start.1 = (bf16[128,768]{1,0:T(8,128)(2,1)}, bf16[128,768]{1,0:T(8,128)(2,1)S(1)}, u32[]{:S(2)}, u32[]{:S(2)}) collective-permute-start(bf16[128,768]{1,0:T(8,128)(2,1)} %param.6), channel_id=1, source_target_pairs={{0,12},{1,13},{2,14},{3,15},{4,0},{5,1},{6,2},{7,3},{8,4},{9,5},{1... | collective-permute-start | bytes 589832 | tf_op jit(solution)/shard_map/ppermute | solution.py:33
  20.6 35.7 %collective-permute-start.3 = (bf16[128,1024]{1,0:T(8,128)(2,1)}, bf16[128,1024]{1,0:T(8,128)(2,1)S(1)}, u32[]{:S(2)}, u32[]{:S(2)}) collective-permute-start(bf16[128,1024]{1,0:T(8,128)(2,1)} %param.7), channel_id=1, source_target_pairs={{0,32},{16,48},{32,0},{48,16},{64,96},{80,112},{96,64},{112,80},{1... | collective-permute-start | bytes 786440 | tf_op jit(solution)/shard_map/ppermute | solution.py:33
  21.3 37.5 %copy-start.16 = (bf16[128,1024]{1,0:T(8,128)(2,1)S(1)}, bf16[128,1024]{1,0:T(8,128)(2,1)}, u32[]{:S(2)}) copy-start(bf16[128,1024]{1,0:T(8,128)(2,1)} %param.7) | copy-start | bytes 786436
  34.7 29.4 %copy-start.14 = (bf16[4,64,768]{2,1,0:T(8,128)(2,1)}, bf16[4,64,768]{2,1,0:T(8,128)(2,1)S(1)}, u32[]{:S(2)}) copy-start(bf16[4,64,768]{2,1,0:T(8,128)(2,1)S(1)} %get-tuple-element.74) | copy-start | bytes 1179652
  34.7 30.7 %collective-permute-start.8 = (bf16[4,64,768]{2,1,0:T(8,128)(2,1)S(1)}, bf16[4,64,768]{2,1,0:T(8,128)(2,1)S(1)}, u32[]{:S(2)}, u32[]{:S(2)}) collective-permute-start(bf16[4,64,768]{2,1,0:T(8,128)(2,1)S(1)} %get-tuple-element.75), channel_id=1, source_target_pairs={{0,2},{1,3},{2,0},{3,1},{4,6},{5,7},{6,4},{7,5},{8,10},{9,11},{10,... | collective-permute-start | bytes 1179656 | tf_op jit(solution)/shard_map/ppermute | solution.py:33
  37.5 27.8 %collective-permute-start.7 = (bf16[4,64,768]{2,1,0:T(8,128)(2,1)S(1)}, bf16[4,64,768]{2,1,0:T(8,128)(2,1)S(1)}, u32[]{:S(2)}, u32[]{:S(2)}) collective-permute-start(bf16[4,64,768]{2,1,0:T(8,128)(2,1)S(1)} %get-tuple-element.75), channel_id=1, source_target_pairs={{0,3},{1,0},{2,1},{3,2},{4,7},{5,4},{6,5},{7,6},{8,11},{9,8},{10,9... | collective-permute-start | bytes 1179656 | tf_op jit(solution)/shard_map/ppermute | solution.py:33
  38.3 26.9 %collective-permute-start.6 = (bf16[4,64,768]{2,1,0:T(8,128)(2,1)S(1)}, bf16[4,64,768]{2,1,0:T(8,128)(2,1)S(1)}, u32[]{:S(2)}, u32[]{:S(2)}) collective-permute-start(bf16[4,64,768]{2,1,0:T(8,128)(2,1)S(1)} %get-tuple-element.75), channel_id=1, source_target_pairs={{0,1},{1,2},{2,3},{3,0},{4,5},{5,6},{6,7},{7,4},{8,9},{9,10},{10,1... | collective-permute-start | bytes 1179656 | tf_op jit(solution)/shard_map/ppermute | solution.py:33
  38.9 21.6 %collective-permute-start.4 = (bf16[128,768]{1,0:T(8,128)(2,1)}, bf16[128,768]{1,0:T(8,128)(2,1)S(1)}, u32[]{:S(2)}, u32[]{:S(2)}) collective-permute-start(bf16[128,768]{1,0:T(8,128)(2,1)} %param.5), channel_id=1, source_target_pairs={{0,4},{1,5},{2,6},{3,7},{4,0},{5,1},{6,2},{7,3},{8,12},{9,13},{10,... | collective-permute-start | bytes 589832 | tf_op jit(solution)/shard_map/ppermute | solution.py:37
  56.3 7.8 %collective-permute-start.5 = (bf16[4,64,768]{2,1,0:T(8,128)(2,1)S(1)}, bf16[4,64,768]{2,1,0:T(8,128)(2,1)S(1)}, u32[]{:S(2)}, u32[]{:S(2)}) collective-permute-start(bf16[4,64,768]{2,1,0:T(8,128)(2,1)S(1)} %get-tuple-element.74), channel_id=1, source_target_pairs={{0,1},{1,0},{2,3},{3,2},{4,5},{5,4},{6,7},{7,6},{8,9},{9,8},{10,11... | collective-permute-start | bytes 1179656 | tf_op jit(solution)/shard_map/ppermute | solution.py:44
  68.4 4.3 %collective-permute-start.9 = (bf16[512,1024]{1,0:T(8,128)(2,1)}, bf16[512,1024]{1,0:T(8,128)(2,1)}, u32[]{:S(2)}, u32[]{:S(2)}) collective-permute-start(bf16[512,1024]{1,0:T(8,128)(2,1)} %convolution_convert_fusion.1), channel_id=1, source_target_pairs={{0,16},{16,0},{32,48},{48,32},{64,80},{80,64},{96,112},{112,96},{1... | collective-permute-start | bytes 3145736 | tf_op jit(solution)/shard_map/ppermute | solution.py:33
  70.1 11.5 %collective-permute-start.10 = (bf16[2,4,64,768]{3,2,1,0:T(8,128)(2,1)}, bf16[2,4,64,768]{3,2,1,0:T(8,128)(2,1)}, u32[]{:S(2)}, u32[]{:S(2)}) collective-permute-start(bf16[2,4,64,768]{3,2,1,0:T(8,128)(2,1)} %pad_maximum_fusion.1), channel_id=1, source_target_pairs={{0,3},{1,2},{2,1},{3,0},{4,7},{5,6},{6,5},{7,4},{8,11},{9,10},{10,... | collective-permute-start | bytes 2359304 | tf_op jit(solution)/shard_map/ppermute | solution.py:44
  83.6 1.2 copy-start.8
  85.9 7.8 %copy-start.18 = (bf16[2,64,1024]{2,1,0:T(8,128)(2,1)S(1)}, bf16[2,64,1024]{2,1,0:T(8,128)(2,1)}, u32[]{:S(2)}) copy-start(bf16[2,64,1024]{2,1,0:T(8,128)(2,1)} %get-tuple-element.62) | copy-start | bytes 786436
  87.9 6.9 %collective-permute-start.11 = (bf16[512,1024]{1,0:T(8,128)(2,1)}, bf16[512,1024]{1,0:T(8,128)(2,1)}, u32[]{:S(2)}, u32[]{:S(2)}) collective-permute-start(bf16[512,1024]{1,0:T(8,128)(2,1)} %convolution_convert_fusion), channel_id=1, source_target_pairs={{0,16},{16,0},{32,48},{48,32},{64,80},{80,64},{96,112},{112,96},{1... | collective-permute-start | bytes 3145736 | tf_op jit(solution)/shard_map/ppermute | solution.py:33
  90.2 9.6 %collective-permute-start.14 = (bf16[2,64,1024]{2,1,0:T(8,128)(2,1)}, bf16[2,64,1024]{2,1,0:T(8,128)(2,1)S(1)}, u32[]{:S(2)}, u32[]{:S(2)}) collective-permute-start(bf16[2,64,1024]{2,1,0:T(8,128)(2,1)} %get-tuple-element.60), channel_id=1, source_target_pairs={{0,128},{16,144},{32,160},{48,176},{64,192},{80,208},{96,224},{112... | collective-permute-start | bytes 786440 | tf_op jit(solution)/shard_map/ppermute | solution.py:33
  90.4 15.3 %collective-permute-start.12 = (bf16[2,64,1024]{2,1,0:T(8,128)(2,1)}, bf16[2,64,1024]{2,1,0:T(8,128)(2,1)S(1)}, u32[]{:S(2)}, u32[]{:S(2)}) collective-permute-start(bf16[2,64,1024]{2,1,0:T(8,128)(2,1)} %get-tuple-element.61), channel_id=1, source_target_pairs={{0,64},{16,80},{32,96},{48,112},{64,128},{80,144},{96,160},{112,17... | collective-permute-start | bytes 786440 | tf_op jit(solution)/shard_map/ppermute | solution.py:33
  93.8 12.3 %collective-permute-start.13 = (bf16[2,64,1024]{2,1,0:T(8,128)(2,1)S(1)}, bf16[2,64,1024]{2,1,0:T(8,128)(2,1)S(1)}, u32[]{:S(2)}, u32[]{:S(2)}) collective-permute-start(bf16[2,64,1024]{2,1,0:T(8,128)(2,1)S(1)} %copy-done.18), channel_id=1, source_target_pairs={{0,192},{16,208},{32,224},{48,240},{64,0},{80,16},{96,32},{112,48}... | collective-permute-start | bytes 786440 | tf_op jit(solution)/shard_map/ppermute | solution.py:33
  97.3 8.8 %copy-start.17 = (f32[512,1024]{1,0:T(8,128)}, f32[512,1024]{1,0:T(8,128)S(1)}, u32[]{:S(2)}) copy-start(f32[512,1024]{1,0:T(8,128)S(1)} %convert_add_fusion.1) | copy-start | bytes 6291460
  97.4 19.1 %copy-start.10 = (f32[2,128,1024]{2,1,0:T(8,128)S(1)}, f32[2,128,1024]{2,1,0:T(8,128)}, u32[]{:S(2)}) copy-start(f32[2,128,1024]{2,1,0:T(8,128)} %fusion.18) | copy-start | bytes 3145732
  106.2 10.2 %collective-permute-start.15 = (bf16[2,64,1024]{2,1,0:T(8,128)(2,1)S(1)}, bf16[2,64,1024]{2,1,0:T(8,128)(2,1)S(1)}, u32[]{:S(2)}, u32[]{:S(2)}) collective-permute-start(bf16[2,64,1024]{2,1,0:T(8,128)(2,1)S(1)} %convert_add_fusion.7), channel_id=1, source_target_pairs={{0,32},{16,48},{32,0},{48,16},{64,96},{80,112},{96,64},{112,80},{1... | collective-permute-start | bytes 786440 | tf_op jit(solution)/shard_map/ppermute | solution.py:33
  106.7 20.7 %collective-permute-start.20 = (bf16[2,128,768]{2,1,0:T(8,128)(2,1)}, bf16[2,128,768]{2,1,0:T(8,128)(2,1)}, u32[]{:S(2)}, u32[]{:S(2)}) collective-permute-start(bf16[2,128,768]{2,1,0:T(8,128)(2,1)} %bitcast_dynamic-update-slice_fusion.9), channel_id=1, source_target_pairs={{0,12},{1,13},{2,14},{3,15},{4,8},{5,9},{6,10},{7,11},{8,4},{9,5},... | collective-permute-start | bytes 1179656 | tf_op jit(solution)/shard_map/ppermute | solution.py:37
  128.4 12.3 %copy-start.6 = (bf16[2,2,128,768]{3,2,1,0:T(8,128)(2,1)}, bf16[2,2,128,768]{3,2,1,0:T(8,128)(2,1)S(1)}, u32[]{:S(2)}) copy-start(bf16[2,2,128,768]{3,2,1,0:T(8,128)(2,1)S(1)} %bitcast_dynamic-update-slice_fusion.2) | copy-start | bytes 2359300
  128.4 12.1 %collective-permute-start.21 = (bf16[4,128,768]{2,1,0:T(8,128)(2,1)S(1)}, bf16[4,128,768]{2,1,0:T(8,128)(2,1)S(1)}, u32[]{:S(2)}, u32[]{:S(2)}) collective-permute-start(bf16[4,128,768]{2,1,0:T(8,128)(2,1)S(1)} %bitcast.203), channel_id=1, source_target_pairs={{0,1},{1,0},{2,3},{3,2},{4,5},{5,4},{6,7},{7,6},{8,9},{9,8},{10,11... | collective-permute-start | bytes 2359304 | tf_op jit(solution)/shard_map/ppermute | solution.py:44
  130.4 10.3 %collective-permute-start.16 = (bf16[2,64,1024]{2,1,0:T(8,128)(2,1)}, bf16[2,64,1024]{2,1,0:T(8,128)(2,1)S(1)}, u32[]{:S(2)}, u32[]{:S(2)}) collective-permute-start(bf16[2,64,1024]{2,1,0:T(8,128)(2,1)} %get-tuple-element.33), channel_id=1, source_target_pairs={{0,64},{16,80},{32,96},{48,112},{64,128},{80,144},{96,160},{112,17... | collective-permute-start | bytes 786440 | tf_op jit(solution)/shard_map/ppermute | solution.py:33
  130.9 14.1 %collective-permute-start.17 = (bf16[2,64,1024]{2,1,0:T(8,128)(2,1)}, bf16[2,64,1024]{2,1,0:T(8,128)(2,1)S(1)}, u32[]{:S(2)}, u32[]{:S(2)}) collective-permute-start(bf16[2,64,1024]{2,1,0:T(8,128)(2,1)} %get-tuple-element.34), channel_id=1, source_target_pairs={{0,192},{16,208},{32,224},{48,240},{64,0},{80,16},{96,32},{112,48}... | collective-permute-start | bytes 786440 | tf_op jit(solution)/shard_map/ppermute | solution.py:33
  133.3 13.7 %collective-permute-start.18 = (bf16[2,64,1024]{2,1,0:T(8,128)(2,1)}, bf16[2,64,1024]{2,1,0:T(8,128)(2,1)S(1)}, u32[]{:S(2)}, u32[]{:S(2)}) collective-permute-start(bf16[2,64,1024]{2,1,0:T(8,128)(2,1)} %get-tuple-element.35), channel_id=1, source_target_pairs={{0,128},{16,144},{32,160},{48,176},{64,192},{80,208},{96,224},{112... | collective-permute-start | bytes 786440 | tf_op jit(solution)/shard_map/ppermute | solution.py:33
  140.5 6.7 %copy-start.12 = (bf16[4,128,768]{2,1,0:T(8,128)(2,1)}, bf16[4,128,768]{2,1,0:T(8,128)(2,1)S(1)}, u32[]{:S(2)}) copy-start(bf16[4,128,768]{2,1,0:T(8,128)(2,1)S(1)} %collective-permute-done.21) | copy-start | bytes 2359300
  140.5 10.0 %copy-start.2 = (bf16[2048,1024]{1,0:T(8,128)(2,1)S(1)}, bf16[2048,1024]{1,0:T(8,128)(2,1)}, u32[]{:S(2)}) copy-start(bf16[2048,1024]{1,0:T(8,128)(2,1)} %all-gather.2.cloned.1.call-done) | copy-start | bytes 12582916
  140.7 31.5 %collective-permute-start.22 = (bf16[2,4,128,768]{3,2,1,0:T(8,128)(2,1)S(1)}, bf16[2,4,128,768]{3,2,1,0:T(8,128)(2,1)S(1)}, u32[]{:S(2)}, u32[]{:S(2)}) collective-permute-start(bf16[2,4,128,768]{3,2,1,0:T(8,128)(2,1)S(1)} %pad_maximum_fusion), channel_id=1, source_target_pairs={{0,3},{1,2},{2,1},{3,0},{4,7},{5,6},{6,5},{7,4},{8,11},{9,10},{10,... | collective-permute-start | bytes 4718600 | tf_op jit(solution)/shard_map/ppermute | solution.py:44
  147.2 22.9 %collective-permute-start.19 = (bf16[2,64,1024]{2,1,0:T(8,128)(2,1)S(1)}, bf16[2,64,1024]{2,1,0:T(8,128)(2,1)S(1)}, u32[]{:S(2)}, u32[]{:S(2)}) collective-permute-start(bf16[2,64,1024]{2,1,0:T(8,128)(2,1)S(1)} %convert_add_fusion.6), channel_id=1, source_target_pairs={{0,32},{16,48},{32,0},{48,16},{64,96},{80,112},{96,64},{112,80},{1... | collective-permute-start | bytes 786440 | tf_op jit(solution)/shard_map/ppermute | solution.py:33
  148.8 6.7 %collective-permute-start.23 = (bf16[2,64,1024]{2,1,0:T(8,128)(2,1)S(1)}, bf16[2,64,1024]{2,1,0:T(8,128)(2,1)S(1)}, u32[]{:S(2)}, u32[]{:S(2)}) collective-permute-start(bf16[2,64,1024]{2,1,0:T(8,128)(2,1)S(1)} %fusion.26), channel_id=1, source_target_pairs={{0,64},{16,208},{32,96},{48,240},{64,0},{80,144},{96,32},{112,176}... | collective-permute-start | bytes 786440 | tf_op jit(solution)/shard_map/ppermute | solution.py:51
  151.1 19.0 %copy-start.11 = (f32[2,128,1024]{2,1,0:T(8,128)S(1)}, f32[2,128,1024]{2,1,0:T(8,128)}, u32[]{:S(2)}) copy-start(f32[2,128,1024]{2,1,0:T(8,128)} %fusion.18) | copy-start | bytes 3145732
  154.7 16.3 %copy-start.7 = (bf16[2,2,128,768]{3,2,1,0:T(8,128)(2,1)S(1)}, bf16[2,2,128,768]{3,2,1,0:T(8,128)(2,1)}, u32[]{:S(2)}) copy-start(bf16[2,2,128,768]{3,2,1,0:T(8,128)(2,1)} %copy-done.6) | copy-start | bytes 2359300
  155.6 22.8 %collective-permute-start.24 = (bf16[2,2,64,1024]{3,2,1,0:T(8,128)(2,1)S(1)}, bf16[2,2,64,1024]{3,2,1,0:T(8,128)(2,1)S(1)}, u32[]{:S(2)}, u32[]{:S(2)}) collective-permute-start(bf16[2,2,64,1024]{3,2,1,0:T(8,128)(2,1)S(1)} %pad_maximum_fusion.2), channel_id=1, source_target_pairs={{0,192},{16,80},{32,224},{48,112},{64,128},{80,16},{96,160},{112,4... | collective-permute-start | bytes 1572872 | tf_op jit(solution)/shard_map/ppermute | solution.py:51
  170.9 1.1 copy-start.13
  179.9 10.1 %collective-permute-start.25 = (bf16[2,4,64,1024]{3,2,1,0:T(8,128)(2,1)}, bf16[2,4,64,1024]{3,2,1,0:T(8,128)(2,1)}, u32[]{:S(2)}, u32[]{:S(2)}) collective-permute-start(bf16[2,4,64,1024]{3,2,1,0:T(8,128)(2,1)} %fusion.41), channel_id=1, source_target_pairs={{0,16},{16,0},{32,48},{48,32},{64,80},{80,64},{96,112},{112,96},{1... | collective-permute-start | bytes 3145736 | tf_op jit(solution)/shard_map/ppermute | solution.py:33
  182.2 6.6 %collective-permute-start.26 = (bf16[2,64,1024]{2,1,0:T(8,128)(2,1)}, bf16[2,64,1024]{2,1,0:T(8,128)(2,1)S(1)}, u32[]{:S(2)}, u32[]{:S(2)}) collective-permute-start(bf16[2,64,1024]{2,1,0:T(8,128)(2,1)} %fusion.25), channel_id=1, source_target_pairs={{0,64},{16,208},{32,96},{48,240},{64,0},{80,144},{96,32},{112,176}... | collective-permute-start | bytes 786440 | tf_op jit(solution)/shard_map/ppermute | solution.py:51
  189.9 3.0 %copy-start.19 = (bf16[768,1024]{1,0:T(8,128)(2,1)S(1)}, bf16[768,1024]{1,0:T(8,128)(2,1)}, u32[]{:S(2)}) copy-start(bf16[768,1024]{1,0:T(8,128)(2,1)} %param.8) | copy-start | bytes 4718596
  189.9 9.0 %collective-permute-start.27 = (bf16[2,2,64,1024]{3,2,1,0:T(8,128)(2,1)S(1)}, bf16[2,2,64,1024]{3,2,1,0:T(8,128)(2,1)S(1)}, u32[]{:S(2)}, u32[]{:S(2)}) collective-permute-start(bf16[2,2,64,1024]{3,2,1,0:T(8,128)(2,1)S(1)} %pad_maximum_fusion.3), channel_id=1, source_target_pairs={{0,192},{16,80},{32,224},{48,112},{64,128},{80,16},{96,160},{112,4... | collective-permute-start | bytes 1572872 | tf_op jit(solution)/shard_map/ppermute | solution.py:51
  192.9 1.9 copy-start.4
  194.8 4.1 %copy-start.15 = (f32[4,4,64,768]{3,2,1,0:T(8,128)}, f32[4,4,64,768]{3,2,1,0:T(8,128)S(1)}, u32[]{:S(2)}) copy-start(f32[4,4,64,768]{3,2,1,0:T(8,128)S(1)} %fusion.11) | copy-start | bytes 9437188
  200.4 4.5 %collective-permute-start.28 = (bf16[2,4,64,1024]{3,2,1,0:T(8,128)(2,1)}, bf16[2,4,64,1024]{3,2,1,0:T(8,128)(2,1)}, u32[]{:S(2)}, u32[]{:S(2)}) collective-permute-start(bf16[2,4,64,1024]{3,2,1,0:T(8,128)(2,1)} %fusion.39), channel_id=1, source_target_pairs={{0,16},{16,0},{32,48},{48,32},{64,80},{80,64},{96,112},{112,96},{1... | collective-permute-start | bytes 3145736 | tf_op jit(solution)/shard_map/ppermute | solution.py:33
  202.2 5.4 %copy-start.20 = (bf16[768,1024]{1,0:T(8,128)(2,1)S(1)}, bf16[768,1024]{1,0:T(8,128)(2,1)}, u32[]{:S(2)}) copy-start(bf16[768,1024]{1,0:T(8,128)(2,1)} %param.8) | copy-start | bytes 4718596
  202.2 19.2 %collective-permute-start.31 = (bf16[4,64,768]{2,1,0:T(8,128)(2,1)}, bf16[4,64,768]{2,1,0:T(8,128)(2,1)S(1)}, u32[]{:S(2)}, u32[]{:S(2)}) collective-permute-start(bf16[4,64,768]{2,1,0:T(8,128)(2,1)} %get-tuple-element.54), channel_id=1, source_target_pairs={{0,2},{1,3},{2,0},{3,1},{4,6},{5,7},{6,4},{7,5},{8,10},{9,11},{10,... | collective-permute-start | bytes 1179656 | tf_op jit(solution)/shard_map/ppermute | solution.py:33
  202.2 19.2 %collective-permute-start.30 = (bf16[4,64,768]{2,1,0:T(8,128)(2,1)}, bf16[4,64,768]{2,1,0:T(8,128)(2,1)S(1)}, u32[]{:S(2)}, u32[]{:S(2)}) collective-permute-start(bf16[4,64,768]{2,1,0:T(8,128)(2,1)} %get-tuple-element.55), channel_id=1, source_target_pairs={{0,3},{1,0},{2,1},{3,2},{4,7},{5,4},{6,5},{7,6},{8,11},{9,8},{10,9... | collective-permute-start | bytes 1179656 | tf_op jit(solution)/shard_map/ppermute | solution.py:33
  203.3 20.1 %collective-permute-start.29 = (bf16[4,64,768]{2,1,0:T(8,128)(2,1)}, bf16[4,64,768]{2,1,0:T(8,128)(2,1)S(1)}, u32[]{:S(2)}, u32[]{:S(2)}) collective-permute-start(bf16[4,64,768]{2,1,0:T(8,128)(2,1)} %get-tuple-element.56), channel_id=1, source_target_pairs={{0,1},{1,2},{2,3},{3,0},{4,5},{5,6},{6,7},{7,4},{8,9},{9,10},{10,1... | collective-permute-start | bytes 1179656 | tf_op jit(solution)/shard_map/ppermute | solution.py:33
  209.5 2.4 copy-start.3
  211.9 1.4 copy-start.9
  211.9 2.4 copy-start.21
  218.0 1.6 copy-start.5
  223.6 30.1 %collective-permute-start.34 = (bf16[64,768]{1,0:T(8,128)(2,1)S(1)}, bf16[64,768]{1,0:T(8,128)(2,1)S(1)}, u32[]{:S(2)}, u32[]{:S(2)}) collective-permute-start(bf16[64,768]{1,0:T(8,128)(2,1)S(1)} %get-tuple-element.70), channel_id=1, source_target_pairs={{0,8},{1,9},{2,10},{3,11},{4,12},{5,13},{6,14},{7,15},{8,0},{9,1},... | collective-permute-start | bytes 294920 | tf_op jit(solution)/shard_map/ppermute | solution.py:33
  226.2 31.0 %collective-permute-start.33 = (bf16[64,768]{1,0:T(8,128)(2,1)S(1)}, bf16[64,768]{1,0:T(8,128)(2,1)S(1)}, u32[]{:S(2)}, u32[]{:S(2)}) collective-permute-start(bf16[64,768]{1,0:T(8,128)(2,1)S(1)} %get-tuple-element.71), channel_id=1, source_target_pairs={{0,12},{1,13},{2,14},{3,15},{4,0},{5,1},{6,2},{7,3},{8,4},{9,5},{1... | collective-permute-start | bytes 294920 | tf_op jit(solution)/shard_map/ppermute | solution.py:33
  226.4 9.9 %collective-permute-start.36 = (bf16[4,64,768]{2,1,0:T(8,128)(2,1)S(1)}, bf16[4,64,768]{2,1,0:T(8,128)(2,1)S(1)}, u32[]{:S(2)}, u32[]{:S(2)}) collective-permute-start(bf16[4,64,768]{2,1,0:T(8,128)(2,1)S(1)} %get-tuple-element.49), channel_id=1, source_target_pairs={{0,3},{1,0},{2,1},{3,2},{4,7},{5,4},{6,5},{7,6},{8,11},{9,8},{10,9... | collective-permute-start | bytes 1179656 | tf_op jit(solution)/shard_map/ppermute | solution.py:33
  227.1 11.2 %collective-permute-start.37 = (bf16[4,64,768]{2,1,0:T(8,128)(2,1)S(1)}, bf16[4,64,768]{2,1,0:T(8,128)(2,1)S(1)}, u32[]{:S(2)}, u32[]{:S(2)}) collective-permute-start(bf16[4,64,768]{2,1,0:T(8,128)(2,1)S(1)} %get-tuple-element.50), channel_id=1, source_target_pairs={{0,2},{1,3},{2,0},{3,1},{4,6},{5,7},{6,4},{7,5},{8,10},{9,11},{10,... | collective-permute-start | bytes 1179656 | tf_op jit(solution)/shard_map/ppermute | solution.py:33
  227.4 20.7 %collective-permute-start.35 = (bf16[4,64,768]{2,1,0:T(8,128)(2,1)S(1)}, bf16[4,64,768]{2,1,0:T(8,128)(2,1)S(1)}, u32[]{:S(2)}, u32[]{:S(2)}) collective-permute-start(bf16[4,64,768]{2,1,0:T(8,128)(2,1)S(1)} %get-tuple-element.48), channel_id=1, source_target_pairs={{0,1},{1,2},{2,3},{3,0},{4,5},{5,6},{6,7},{7,4},{8,9},{9,10},{10,1... | collective-permute-start | bytes 1179656 | tf_op jit(solution)/shard_map/ppermute | solution.py:33
  231.6 34.0 %copy-start.1 = (bf16[1024,768]{1,0:T(8,128)(2,1)S(1)}, bf16[1024,768]{1,0:T(8,128)(2,1)}, u32[]{:S(2)}) copy-start(bf16[1024,768]{1,0:T(8,128)(2,1)} %param.9) | copy-start | bytes 4718596
  236.4 20.9 %collective-permute-start.32 = (bf16[64,768]{1,0:T(8,128)(2,1)S(1)}, bf16[64,768]{1,0:T(8,128)(2,1)S(1)}, u32[]{:S(2)}, u32[]{:S(2)}) collective-permute-start(bf16[64,768]{1,0:T(8,128)(2,1)S(1)} %get-tuple-element.72), channel_id=1, source_target_pairs={{0,4},{1,5},{2,6},{3,7},{4,8},{5,9},{6,10},{7,11},{8,12},{9,13},{1... | collective-permute-start | bytes 294920 | tf_op jit(solution)/shard_map/ppermute | solution.py:33
  248.3 9.0 %collective-permute-start.38 = (bf16[64,768]{1,0:T(8,128)(2,1)S(1)}, bf16[64,768]{1,0:T(8,128)(2,1)S(1)}, u32[]{:S(2)}, u32[]{:S(2)}) collective-permute-start(bf16[64,768]{1,0:T(8,128)(2,1)S(1)} %get-tuple-element.67), channel_id=1, source_target_pairs={{0,4},{1,5},{2,6},{3,7},{4,8},{5,9},{6,10},{7,11},{8,12},{9,13},{1... | collective-permute-start | bytes 294920 | tf_op jit(solution)/shard_map/ppermute | solution.py:33
  250.7 7.5 %collective-permute-start.40 = (bf16[64,768]{1,0:T(8,128)(2,1)S(1)}, bf16[64,768]{1,0:T(8,128)(2,1)S(1)}, u32[]{:S(2)}, u32[]{:S(2)}) collective-permute-start(bf16[64,768]{1,0:T(8,128)(2,1)S(1)} %get-tuple-element.68), channel_id=1, source_target_pairs={{0,8},{1,9},{2,10},{3,11},{4,12},{5,13},{6,14},{7,15},{8,0},{9,1},... | collective-permute-start | bytes 294920 | tf_op jit(solution)/shard_map/ppermute | solution.py:33
  253.8 11.1 %collective-permute-start.39 = (bf16[64,768]{1,0:T(8,128)(2,1)S(1)}, bf16[64,768]{1,0:T(8,128)(2,1)S(1)}, u32[]{:S(2)}, u32[]{:S(2)}) collective-permute-start(bf16[64,768]{1,0:T(8,128)(2,1)S(1)} %get-tuple-element.69), channel_id=1, source_target_pairs={{0,12},{1,13},{2,14},{3,15},{4,0},{5,1},{6,2},{7,3},{8,4},{9,5},{1... | collective-permute-start | bytes 294920 | tf_op jit(solution)/shard_map/ppermute | solution.py:33
Sparse Core Ops, SparseCore 0:
  9.9 62.6 all-gather.1
